TPU v7x, 512 devices: a whole 4x8x8 slice. The times are simulated.
512 devices in a mesh: seq: 16 (over y, core), ep: 32 (over z, x).
Axes of the slice: x: 4, y: 8, z: 8, core: 2. Of those that a mesh axis runs over, the one named last changes fastest.
Arguments:
- latent: bfloat16 [256, 2048, 576], P('ep', 'seq'), may hold values from -6 to 6
- lengths: int32 [32, 8], P('ep'), may hold values from 1 to 2048, 13107 in all within a row
- queries: bfloat16 [256, 128, 576], P('ep', 'seq'), may hold values from -30 to 30
- fresh_latent: bfloat16 [256, 576], P('ep'), may hold values from -7 to 7
- tokens: bfloat16 [1024, 3584], P('ep', 'seq'), may hold values from -6 to 6
- routes: int32 [1024, 8], P('ep'), may hold values from 0 to 31, all different within a row; in each aligned block of 32 rows (0 to 31, 32 to 63, ...) at most 16 rows name the same one
- gates: float32 [1024, 8], P('ep'), may hold values from 0.05 to 0.5
- w_gate: bfloat16 [32, 3584, 2048], P('ep', None, 'seq'), may hold values from -0.09375 to 0.09375
- w_up: bfloat16 [32, 3584, 2048], P('ep', None, 'seq'), may hold values from -0.09375 to 0.09375
- w_down: bfloat16 [32, 2048, 3584], P('ep', 'seq'), may hold values from -0.125 to 0.125
Outputs:
- context: bfloat16 [256, 128, 512], P('ep', 'seq')
- mixed_out: bfloat16 [1024, 3584], P('ep', 'seq')
Inputs may be any that keep to these rules, and one draw needn't show every extreme that they name: `routes`: in the 32 tokens of one index of ep no expert is named more than 16 times. Each row of 8 lengths sums to 13107.
All inputs are finite; a program needn't handle non-finite values.
Results may differ from a plain program's by a relative error of at most 0.025.
Values may be sent and summed in bfloat16 or wider, within the bound.
A program may use at most 128 MiB of HBM per device.

v0:
```python
import jax
import jax.numpy as jnp
from jax import lax
from jax.sharding import PartitionSpec as P

LAT = 512


score_scale = 0.07216878364870322
neg_fill = -1e30


def slot_table(route_rows, experts, capacity):
    flat_rows = route_rows.reshape(-1)
    one_hot = (flat_rows[:, None] == jnp.arange(experts, dtype=jnp.int32)[None, :]).astype(
        jnp.int32
    )
    before = jnp.cumsum(one_hot, axis=0) - one_hot
    position = jnp.sum(before * one_hot, axis=1)
    return (flat_rows * capacity + position).reshape(route_rows.shape)


def attend(query_rows, cache_rows, fresh_key, length):
    scores = (
        jnp.einsum("hc,sc->hs", query_rows, cache_rows, preferred_element_type=jnp.float32)
        * score_scale
    )
    position = jnp.arange(cache_rows.shape[0], dtype=jnp.int32)
    scores = jnp.where(position[None, :] < length, scores, neg_fill)
    own_score = jnp.dot(query_rows, fresh_key, preferred_element_type=jnp.float32) * score_scale
    highest = jnp.maximum(jnp.max(scores, axis=1), own_score)
    weights = jnp.exp(scores - highest[:, None])
    own_weight = jnp.exp(own_score - highest)
    totals = jnp.sum(weights, axis=1) + own_weight
    probability = (weights / totals[:, None]).astype(jnp.bfloat16)
    own_prob = (own_weight / totals).astype(jnp.bfloat16)
    summed = jnp.dot(probability, cache_rows[:, :LAT], preferred_element_type=jnp.float32)
    summed = (
        summed
        + own_prob.astype(jnp.float32)[:, None] * fresh_key[:LAT].astype(jnp.float32)[None, :]
    )
    return summed.astype(jnp.bfloat16)


def on_device(latent, lengths, queries, fresh_latent, tokens, routes, gates, w_gate, w_up, w_down):
    seq_count = lax.axis_size("seq")
    my_index = lax.axis_index("seq")
    req_count = latent.shape[0]
    head_share = queries.shape[1]
    length_row = lengths[0]
    all_heads = lax.all_gather(queries, "seq", axis=1, tiled=True)
    owner_row = 2 * jnp.arange(req_count, dtype=jnp.int32)
    chooser = (owner_row[None, :] == jnp.arange(seq_count, dtype=jnp.int32)[:, None]).astype(
        jnp.bfloat16
    )
    outgoing = jnp.einsum(
        "or,rsc->osc", chooser, latent, preferred_element_type=jnp.float32
    ).astype(jnp.bfloat16)
    arrived = lax.all_to_all(outgoing, "seq", split_axis=0, concat_axis=0, tiled=True)
    cache_rows = arrived.reshape(-1, arrived.shape[-1])
    owned = owner_row == my_index
    owned_mask = owned.astype(jnp.bfloat16)
    query_rows = jnp.einsum(
        "r,rhc->hc", owned_mask, all_heads, preferred_element_type=jnp.float32
    ).astype(jnp.bfloat16)
    fresh_key = jnp.dot(owned_mask, fresh_latent, preferred_element_type=jnp.float32).astype(
        jnp.bfloat16
    )
    length = jnp.sum(jnp.where(owned, length_row, 0))
    decoded = attend(query_rows, cache_rows, fresh_key, length)
    spread = lax.all_to_all(
        decoded.reshape(seq_count, head_share, -1), "seq", split_axis=0, concat_axis=0, tiled=True
    )
    context = jnp.einsum(
        "ro,ohl->rhl", jnp.transpose(chooser), spread, preferred_element_type=jnp.float32
    ).astype(jnp.bfloat16)
    ep_count = lax.axis_size("ep")
    tok_rows = tokens.shape[0]
    local_experts = w_gate.shape[0]
    experts = local_experts * ep_count
    capacity = tok_rows // 2
    slot_ids = slot_table(routes, experts, capacity)
    every_slot = jnp.arange(experts * capacity, dtype=jnp.int32)
    matches = slot_ids[:, :, None] == every_slot[None, None, :]
    dispatch_matrix = jnp.transpose(jnp.any(matches, axis=1)).astype(jnp.bfloat16)
    combine_matrix = jnp.sum(jnp.where(matches, gates[:, :, None], 0.0), axis=1)
    placed = jnp.dot(dispatch_matrix, tokens, preferred_element_type=jnp.float32).astype(
        jnp.bfloat16
    )
    arrived_rows = lax.all_to_all(
        placed.reshape(ep_count, local_experts * capacity, -1),
        "ep",
        split_axis=0,
        concat_axis=0,
        tiled=True,
    )
    slot_block = lax.all_gather(arrived_rows, "seq", axis=2, tiled=True)
    width = slot_block.shape[-1]
    moved = slot_block.reshape(ep_count, local_experts, capacity, width).transpose(1, 0, 2, 3)
    expert_rows = moved.reshape(local_experts, ep_count * capacity, width)
    gate_add = jnp.einsum("erd,edf->erf", expert_rows, w_gate, preferred_element_type=jnp.float32)
    up_add = jnp.einsum("erd,edf->erf", expert_rows, w_up, preferred_element_type=jnp.float32)
    hidden = (jax.nn.silu(gate_add) * up_add).astype(jnp.bfloat16)
    partial_out = jnp.einsum("erf,efd->erd", hidden, w_down, preferred_element_type=jnp.float32)
    width = partial_out.shape[-1]
    moved = partial_out.reshape(local_experts, ep_count, capacity, width).transpose(1, 0, 2, 3)
    block_sums = lax.psum_scatter(
        moved.reshape(ep_count, local_experts * capacity, width).astype(jnp.bfloat16),
        "seq",
        scatter_dimension=2,
        tiled=True,
    )
    returned = lax.all_to_all(block_sums, "ep", split_axis=0, concat_axis=0, tiled=True)
    flat_rows = returned.reshape(experts * capacity, -1).astype(jnp.float32)
    mixed_out = jnp.dot(combine_matrix, flat_rows, precision=lax.Precision.HIGHEST).astype(
        jnp.bfloat16
    )
    return (context, mixed_out)


def solution(mesh):
    placed = (
        P("ep", "seq", None),
        P("ep", None),
        P("ep", "seq", None),
        P("ep", None),
        P("ep", "seq"),
        P("ep", None),
        P("ep", None),
        P("ep", None, "seq"),
        P("ep", None, "seq"),
        P("ep", "seq", None),
    )
    return jax.shard_map(
        on_device,
        mesh=mesh,
        in_specs=placed,
        out_specs=(P("ep", "seq", None), P("ep", "seq")),
        check_vma=False,
    )
```

profile of v0, /device:TPU:1, one launch (start us, length us, event | category | flops | bytes accessed | tf_op | source)
XLA Modules:
  0.0 355.4 jit_solution(3801181642114418407)
XLA Ops:
  7.2 0.8 copy.55
  8.1 0.1 eq.72
  8.2 0.1 eq.68
  8.3 0.6 reduce-window.6
  8.9 0.2 slice_reduce_fusion
  9.1 0.1 fusion.28
  9.3 0.2 fusion.20
  9.5 1.0 convolution_convert_fusion.2
  10.5 0.1 copy.60
  10.7 24.7 %all_to_all.20 = bf16[32,16,224]{2,1,0:T(8,128)(2,1)S(1)} all-to-all(bf16[32,16,224]{2,1,0:T(8,128)(2,1)S(1)} %bitcast.79), channel_id=1, replica_groups=mesh['seq'=16,'ep'=32] {'ep'}, dimensions={0} | all-to-all | bytes 458752 | tf_op jit(solution)/shard_map/all_to_all | solution.py:90
  35.4 1.8 copy.61
  37.2 0.7 all-gather.3.cloned.1.call-update
  38.0 85.0 %all-gather.5.cloned.1.call-done = bf16[32,16,3584]{0,1,2:T(8,128)(2,1)} async-done(((bf16[32,16,224]{0,1,2:T(8,128)(2,1)}), bf16[32,16,3584]{0,1,2:T(8,128)(2,1)}) %all-gather.5.cloned.1.call-update) | async-done | bytes 3670032 | tf_op jit(solution)/shard_map/all_gather | solution.py:97
  122.9 17.5 %copy.62 = bf16[32,16,3584]{2,1,0:T(8,128)(2,1)} copy(bf16[32,16,3584]{0,1,2:T(8,128)(2,1)} %all-gather.5.cloned.1.call-done) | data formatting | bytes 7340032 | tf_op jit(solution)/shard_map/all_gather | solution.py:97
  140.5 3.3 fusion.18
  143.8 0.1 copy-done.10
  143.9 1.1 fusion.7
  145.1 2.9 convolution_convert_fusion
  148.0 25.5 %copy.67 = bf16[32,16,3584]{1,0,2:T(8,128)(2,1)} copy(bf16[32,16,3584]{2,1,0:T(8,128)(2,1)} %convolution_convert_fusion) | data formatting | bytes 7340032
  173.5 48.8 %reshape.101 = bf16[3584,512]{1,0:T(8,128)(2,1)} reshape(bf16[3584,32,16]{2,1,0:T(8,128)(2,1)} %bitcast.74) | data formatting | bytes 7340032
  222.3 0.5 copy-done.8
  222.8 3.7 %convolution_convert_fusion.1 = bf16[16,128,576]{1,0,2:T(8,128)(2,1)S(1)} fusion(bf16[8,128,576]{1,2,0:T(8,128)(2,1)S(1)} %copy-done, s32[8]{0:T(128)S(1)} %iota_multiply_fusion), kind=kOutput, calls=%fused_computation.7 | convolution fusion | flops 20054144 | bytes 3538976 | tf_op jit(solution)/shard_map/or,rsc->osc/dot_general | solution.py:56
  226.6 2.0 copy.52
  228.6 4.7 %all-to-all-start = ((bf16[16,128,576]{1,2,0:T(8,128)(2,1)}), bf16[16,128,576]{1,2,0:T(8,128)(2,1)S(1)}, u32[]{:S(2)}, u32[]{:S(2)}) async-start(bf16[16,128,576]{1,2,0:T(8,128)(2,1)} %copy.52), calls=%async_computation | async-start | bytes 4718592 | tf_op jit(solution)/shard_map/all_to_all | solution.py:59
  233.3 0.8 convolution_reduce_fusion
  234.1 0.6 reshape.98
  234.7 0.6 fusion.37
  235.3 1.3 fusion.36
  236.6 1.1 iota_compare_fusion.3
  237.8 0.6 slice_convert_fusion
  238.3 2.4 multiply_reduce_fusion
  240.7 56.2 %all-to-all-done = bf16[16,128,576]{1,2,0:T(8,128)(2,1)S(1)} async-done(((bf16[16,128,576]{1,2,0:T(8,128)(2,1)}), bf16[16,128,576]{1,2,0:T(8,128)(2,1)S(1)}, u32[]{:S(2)}, u32[]{:S(2)}) %all-to-all-start) | async-done | bytes 2359328 | tf_op jit(solution)/shard_map/all_to_all | solution.py:59
  296.9 1.6 fusion.40
  298.6 0.1 fusion.41
  298.7 0.4 fusion.15
  299.1 0.4 copy_bitcast_fusion
  299.5 0.3 copy-done.7
  299.8 1.5 fusion.11
  301.3 4.8 %all-to-all-start.1 = ((bf16[16,8,512]{2,1,0:T(8,128)(2,1)}), bf16[16,8,512]{2,1,0:T(8,128)(2,1)S(1)}, u32[]{:S(2)}, u32[]{:S(2)}) async-start(bf16[16,8,512]{2,1,0:T(8,128)(2,1)} %fusion.11), calls=%async_computation.1 | async-start | bytes 262144 | tf_op jit(solution)/shard_map/all_to_all | solution.py:71
  306.1 17.1 %reduce-scatter.4.cloned.1.call-done = bf16[224,512]{1,0:T(8,128)(2,1)} async-done(((bf16[3584,512]{1,0:T(8,128)(2,1)}), bf16[224,512]{1,0:T(8,128)(2,1)}) %reduce-scatter.4.cloned.1.call-update) | async-done | bytes 229392
  323.1 2.4 reshape.102
  325.5 2.1 copy.68
  327.7 9.9 %all-to-all-start.3 = ((bf16[32,16,224]{2,1,0:T(8,128)(2,1)}), bf16[32,16,224]{2,1,0:T(8,128)(2,1)S(1)}, u32[]{:S(2)}, u32[]{:S(2)}) async-start(bf16[32,16,224]{2,1,0:T(8,128)(2,1)} %copy.68), calls=%async_computation.3 | async-start | bytes 524288 | tf_op jit(solution)/shard_map/all_to_all | solution.py:113
  337.7 0.2 select_reduce_fusion
  337.9 0.2 convolution_convert_fusion.3
  338.1 0.7 copy.63
  338.8 9.3 %all-to-all-done.3 = bf16[32,16,224]{2,1,0:T(8,128)(2,1)S(1)} async-done(((bf16[32,16,224]{2,1,0:T(8,128)(2,1)}), bf16[32,16,224]{2,1,0:T(8,128)(2,1)S(1)}, u32[]{:S(2)}, u32[]{:S(2)}) %all-to-all-start.3) | async-done | bytes 229408 | tf_op jit(solution)/shard_map/all_to_all | solution.py:113
  348.0 0.9 convolution_convert_fusion.4
  (34 shorter events, 0.5 us)
Async XLA Ops:
  7.2 215.7 %copy-start = (bf16[8,128,576]{1,2,0:T(8,128)(2,1)S(1)}, bf16[8,128,576]{1,2,0:T(8,128)(2,1)}, u32[]{:S(2)}) copy-start(bf16[8,128,576]{1,2,0:T(8,128)(2,1)} %param.10) | copy-start | bytes 3538948
  7.2 115.8 %all-gather.5.cloned.1.call-start = ((), (), s32[]{:S(2)}) async-start(), calls=%async_computation.6 | async-start | bytes 15597568 | tf_op jit(solution)/shard_map/all_gather | solution.py:97
  37.1 201.2 %all-gather.3.cloned.1.call-start = ((), (), s32[]{:S(2)}) async-start(), calls=%async_computation.5 | async-start | bytes 1392640 | tf_op jit(solution)/shard_map/all_gather | solution.py:51
  37.9 102.6 %copy-start.2 = (bf16[1,3584,128]{2,1,0:T(8,128)(2,1)S(1)}, bf16[1,3584,128]{2,1,0:T(8,128)(2,1)}, u32[]{:S(2)}) copy-start(bf16[1,3584,128]{2,1,0:T(8,128)(2,1)} %param.17) | copy-start | bytes 2752516
  37.9 285.2 %reduce-scatter.4.cloned.1.call-start = ((), (), s32[]{:S(2)}) async-start(), calls=%async_computation.7 | async-start | bytes 3899392
  140.5 3.4 copy-start.1
  140.5 3.4 copy-start.10
  143.9 1.2 copy-start.3
  222.3 0.5 copy-start.8
  228.6 68.3 %all-to-all-start = ((bf16[16,128,576]{1,2,0:T(8,128)(2,1)}), bf16[16,128,576]{1,2,0:T(8,128)(2,1)S(1)}, u32[]{:S(2)}, u32[]{:S(2)}) async-start(bf16[16,128,576]{1,2,0:T(8,128)(2,1)} %copy.52), calls=%async_computation | async-start | bytes 4718592 | tf_op jit(solution)/shard_map/all_to_all | solution.py:59
  296.9 1.7 copy-start.4
  296.9 1.7 copy-start.5
  299.1 0.7 copy-start.7
  301.3 26.4 %all-to-all-start.1 = ((bf16[16,8,512]{2,1,0:T(8,128)(2,1)}), bf16[16,8,512]{2,1,0:T(8,128)(2,1)S(1)}, u32[]{:S(2)}, u32[]{:S(2)}) async-start(bf16[16,8,512]{2,1,0:T(8,128)(2,1)} %fusion.11), calls=%async_computation.1 | async-start | bytes 262144 | tf_op jit(solution)/shard_map/all_to_all | solution.py:71
  306.0 31.6 %copy-start.6 = (f32[32,8]{0,1:T(8,128)S(1)}, f32[32,8]{0,1:T(8,128)}, u32[]{:S(2)}) copy-start(f32[32,8]{0,1:T(8,128)} %param.16) | copy-start | bytes 3076
  306.0 31.9 %copy-start.9 = (s32[8]{0:T(128)S(1)}, s32[8]{0:T(128)}, u32[]{:S(2)}) copy-start(s32[8]{0:T(128)} %copy-done.8) | copy-start | bytes 100
  327.7 20.4 %all-to-all-start.3 = ((bf16[32,16,224]{2,1,0:T(8,128)(2,1)}), bf16[32,16,224]{2,1,0:T(8,128)(2,1)S(1)}, u32[]{:S(2)}, u32[]{:S(2)}) async-start(bf16[32,16,224]{2,1,0:T(8,128)(2,1)} %copy.68), calls=%async_computation.3 | async-start | bytes 524288 | tf_op jit(solution)/shard_map/all_to_all | solution.py:113
Sparse Core Ops, SparseCore 0:
  37.3 85.6 all-gather.4
  125.0 40.0 all-gather.2
  222.4 100.6 reduce-scatter.3
where the time goes:
time: 361 us; the launch traced here: 355 us
  waiting for transfers between devices  168 us (47%)
  local copies, waits for them, and re-layouts  104 us (29%)
  blocking collectives  24.7 us (7%)
  starting transfers between devices  19.5 us (5%)
  matrix products  17.2 us (5%)
  between operations  14 us (4%)
  other arithmetic  7.54 us (2%)
    all_gather x1, waiting for transfers between devices, on_device(): slot_block = lax.all_gather(arrived_rows, 'seq', axis=2, tiled=True)  85 us
    unnamed x29, local copies, waits for them, and re-layouts  81.4 us
    all_to_all x1, waiting for transfers between devices, on_device(): lax.all_to_all(outgoing, 'seq', split_axis=0, concat_axis=0, tiled=True)  56.2 us
    all_to_all x1, blocking collectives, on_device(): lax.all_to_all(placed.reshape(ep_count, local_experts * capacity, -1), 'e...  24.7 us
    unnamed x4, waiting for transfers between devices  17.8 us
    all_gather x1, local copies, waits for them, and re-layouts, on_device(): slot_block = lax.all_gather(arrived_rows, 'seq', axis=2, tiled=True)  17.5 us
    all_to_all x1, starting transfers between devices, on_device(): lax.all_to_all(block_sums, 'ep', split_axis=0, concat_axis=0, tiled=True)  9.9 us
    all_to_all x1, waiting for transfers between devices, on_device(): lax.all_to_all(block_sums, 'ep', split_axis=0, concat_axis=0, tiled=True)  9.25 us
  transfers between devices with their start and end apart: 6, of which 4 were waited for; matrix products, arithmetic and copies ran while one was open for 34% of the time, Pallas kernels for 0%

commit v1 on v0

v1 whole, which is shorter than its diff:
```python
import functools
import heapq

import jax
import jax.numpy as jnp
from jax import lax
from jax.experimental import pallas as pl
from jax.experimental.pallas import tpu as pltpu
from jax.sharding import PartitionSpec as P

MESH = pl.DeviceIdType.MESH
LAT = 512
NX = 4
LANE = 128
HALF_TOK = 16
SCALE = 0.07216878364870322
NEG = -1.0e30
F32 = jnp.float32
BF16 = jnp.bfloat16

LINK_RATE = 45.0e3
HOP = 1.5


def mod(value, n):
    return lax.rem(value + n, n)


class Net:
    def __init__(self, send, recv):
        self.send, self.recv = send, recv
        self.count, self.now = 0, 0.0
        self.links, self.copies = {}, []

    def copy(self, src, dst, device, link):
        at = self.count
        self.count += 1
        made = pltpu.make_async_remote_copy(
            src_ref=src,
            dst_ref=dst,
            send_sem=self.send.at[at],
            recv_sem=self.recv.at[at],
            device_id=device,
            device_id_type=MESH,
        )
        made.start()
        size = 2
        for extent in src.shape:
            size *= extent
        begin = max(self.links.get(link, 0.0), self.now)
        self.links[link] = begin + size / LINK_RATE
        self.copies.append(made)
        return made, self.links[link] + HOP

    def run(self, tasks):
        heap, order = [], 0
        for task in tasks:
            heap.append((self.now, order, task))
            order += 1
        heapq.heapify(heap)
        while heap:
            at, _, task = heapq.heappop(heap)
            self.now = max(self.now, at)
            try:
                ready = next(task)
            except StopIteration:
                continue
            order += 1
            heapq.heappush(heap, (ready, order, task))


def ring_gather(net, piece, cut, pos, n, device, axis, landed):
    far = n // 2
    up, down = device(mod(pos + 1, n)), device(mod(pos - 1, n))

    def part(ref, side, step):
        return cut(ref, side) if step == far else ref

    own = piece(pos)
    first = part(own, 0, 1)
    cu, tu = net.copy(first, first, up, axis + "+")
    first = part(own, 1, 1)
    cd, td = net.copy(first, first, down, axis + "-")
    landed(pos)
    for k in range(1, far):
        yield tu
        cu.wait_recv()
        at = mod(pos - k, n)
        src = part(piece(at), 0, k + 1)
        cu, tu = net.copy(src, src, up, axis + "+")
        landed(at)
        yield td
        cd.wait_recv()
        at = mod(pos + k, n)
        src = part(piece(at), 1, k + 1)
        cd, td = net.copy(src, src, down, axis + "-")
        landed(at)
    yield max(tu, td)
    cu.wait_recv()
    cd.wait_recv()
    landed(mod(pos + far, n))


def add_into(ref, other):
    ref[...] = (ref[...].astype(F32) + other[...].astype(F32)).astype(BF16)


def ring_scatter(net, piece, cut, arrived, pos, n, device, axis, ready, finish):
    far = n // 2
    up, down = device(mod(pos + 1, n)), device(mod(pos - 1, n))
    while not ready(far):
        yield net.now + 0.01
    src = cut(piece(mod(pos + far, n)), 0)
    cu, tu = net.copy(src, cut(arrived(0, 0), 0), up, axis + "+")
    src = cut(piece(mod(pos + far, n)), 1)
    cd, td = net.copy(src, cut(arrived(1, 0), 1), down, axis + "-")
    for k in range(1, far):
        d = far - k
        while not (ready(d) and ready(-d)):
            yield net.now + 0.01
        yield tu
        cu.wait_recv()
        mine, came = piece(mod(pos + d, n)), arrived(0, k - 1)
        if k == 1:
            add_into(cut(mine, 0), cut(came, 0))
        else:
            add_into(mine, came)
        cu, tu = net.copy(mine, arrived(0, k), up, axis + "+")
        yield td
        cd.wait_recv()
        mine, came = piece(mod(pos - d, n)), arrived(1, k - 1)
        if k == 1:
            add_into(cut(mine, 1), cut(came, 1))
        else:
            add_into(mine, came)
        cd, td = net.copy(mine, arrived(1, k), down, axis + "-")
    while not ready(0):
        yield net.now + 0.01
    yield max(tu, td)
    cu.wait_recv()
    cd.wait_recv()
    if far > 1:
        total = (
            piece(pos)[...].astype(F32)
            + arrived(0, far - 1)[...].astype(F32)
            + arrived(1, far - 1)[...].astype(F32)
        )
        finish(total)
    else:
        add_into(cut(piece(pos), 0), cut(arrived(0, 0), 0))
        add_into(cut(piece(pos), 1), cut(arrived(1, 0), 1))
        finish(piece(pos)[...].astype(F32))


def kernel(
    cfg,
    latent, queries, wg, wu, wd, lengths, fresh, tokens, routes, gates,
    ctx_out, mix_out,
    tokpad, tokbuf, line, xa, xb, wcat, wdcat, acc, hid, ya, yb,
    ra, rax, rbx, rb, ebuf, erecv,
    lbuf, qbuf, qf, obuf, orecv, cf, cb, crecv,
    local_sem, send_sem, recv_sem, t_send, t_recv, q_send, q_recv, e_send, e_recv,
):
    n_seq, n_z, wide_a, wide_b, share, heads = cfg
    n_y = n_seq // 2
    s, e = lax.axis_index("seq"), lax.axis_index("ep")
    y, c = s // 2, lax.rem(s, 2)
    z, x = e // NX, lax.rem(e, NX)
    other = 1 - c
    sibling = (2 * y + other, e)
    experts = n_z * NX
    rows = experts * HALF_TOK
    n_req = lengths.shape[1]
    half_req = n_req // 2
    q_rows = half_req * heads

    def at_x(i):
        return (s, z * NX + i)

    def at_z(i):
        return (s, i * NX + x)

    def local(src, dst, i):
        made = pltpu.make_async_copy(src, dst, local_sem.at[i])
        made.start()
        return made

    mine_q = queries.at[pl.ds(pl.multiple_of(c * q_rows, q_rows), q_rows)]
    loads = [
        local(mine_q, qbuf.at[s], 0),
        local(latent.at[pl.ds(c * half_req, half_req)], lbuf.at[0], 1),
        local(wg, wcat.at[:, pl.ds(0, LANE)], 2),
        local(wu, wcat.at[:, pl.ds(2 * LANE, LANE)], 3),
        local(wd, wdcat.at[pl.ds(0, LANE)], 4),
    ]
    for half in range(2):
        tokpad[half] = jnp.zeros_like(tokpad[half])
        tokpad[half, :, 0:share] = tokens[half * HALF_TOK:(half + 1) * HALF_TOK, :]

    barrier = pltpu.get_barrier_semaphore()

    def greet(j, carry):
        pl.semaphore_signal(
            barrier, inc=1, device_id=(lax.rem(s + j, n_seq), e), device_id_type=MESH
        )
        return carry

    lax.fori_loop(1, n_seq, greet, 0)
    for who in (at_x(mod(x + 1, NX)), at_x(mod(x - 1, NX)), at_z(mod(z + 1, n_z)), at_z(mod(z - 1, n_z))):
        pl.semaphore_signal(barrier, inc=1, device_id=who, device_id_type=MESH)
    pl.semaphore_wait(barrier, n_seq - 1 + 4)

    def token_copy(j):
        to = lax.rem(s + j, n_seq)
        return pltpu.make_async_remote_copy(
            src_ref=tokpad.at[lax.rem(to, 2)],
            dst_ref=tokbuf.at[s],
            send_sem=t_send.at[j],
            recv_sem=t_recv.at[j],
            device_id=(to, e),
            device_id_type=MESH,
        )

    def query_copy(j):
        to = lax.rem(s + j, n_seq)
        begin = pl.multiple_of(lax.rem(to, 2) * q_rows, q_rows)
        return pltpu.make_async_remote_copy(
            src_ref=queries.at[pl.ds(begin, q_rows)],
            dst_ref=qbuf.at[s],
            send_sem=q_send.at[j],
            recv_sem=q_recv.at[j],
            device_id=(to, e),
            device_id_type=MESH,
        )

    def end_copy(j):
        to = lax.rem(s + j, n_seq)
        return pltpu.make_async_remote_copy(
            src_ref=ebuf.at[to],
            dst_ref=erecv.at[s],
            send_sem=e_send.at[j],
            recv_sem=e_recv.at[j],
            device_id=(to, e),
            device_id_type=MESH,
        )

    def each(act):
        def body(j, carry):
            act(j)
            return carry

        lax.fori_loop(1, n_seq, body, 0)

    net = Net(send_sem, recv_sem)
    each(lambda j: token_copy(j).start())
    each(lambda j: query_copy(j).start())
    lat_copy, _ = net.copy(latent.at[pl.ds(other * half_req, half_req)], lbuf.at[1], sibling, "core")
    wg_copy, _ = net.copy(wg, wcat.at[:, pl.ds(LANE, LANE)], sibling, "core")
    wu_copy, _ = net.copy(wu, wcat.at[:, pl.ds(3 * LANE, LANE)], sibling, "core")
    wd_copy, _ = net.copy(wd, wdcat.at[pl.ds(LANE, LANE)], sibling, "core")

    first_row = pl.multiple_of(c * HALF_TOK, HALF_TOK)
    my_routes = routes[pl.ds(first_row, HALF_TOK), :]
    my_gates = gates[pl.ds(first_row, HALF_TOK), :]
    lane = lax.broadcasted_iota(jnp.int32, (HALF_TOK, LANE), 1)
    named = jnp.where(lane < experts, lane, lane - experts)
    weight = jnp.zeros((HALF_TOK, LANE), F32)
    for k in range(my_routes.shape[1]):
        weight = weight + jnp.where(named == my_routes[:, k:k + 1], my_gates[:, k:k + 1], 0.0)
    high = weight.astype(BF16).astype(F32)
    weight = jnp.where(lane < experts, high, jnp.where(lane < 2 * experts, weight - high, 0.0))

    tokbuf[s] = tokpad[c]
    line[...] = jnp.zeros_like(line)
    each(lambda j: token_copy(j).wait_recv())
    for i in range(n_seq):
        begin, turn = share * i // LANE * LANE, share * i % LANE
        span = tokpad.shape[2] + LANE
        value = jnp.concatenate(
            [tokbuf[i].astype(F32), jnp.zeros((HALF_TOK, LANE), F32)], axis=1
        )
        if turn:
            value = pltpu.roll(value, turn, 1)
        line[:, begin:begin + span] = line[:, begin:begin + span] + value
    xa[z, x] = line[:, 0:wide_a].astype(BF16)
    xb[z, x, :, 0:wide_b] = line[:, wide_a:wide_a + wide_b].astype(BF16)
    xb[z, x, :, wide_b:wide_b + LANE] = weight.astype(BF16)

    position = lax.broadcasted_iota(jnp.int32, (n_seq * heads, LANE), 1)

    def attend():
        yield net.now + 5.0
        loads[0].wait()
        loads[1].wait()
        each(lambda j: query_copy(j).wait_recv())
        lat_copy.wait_recv()
        qf[...] = qbuf[...].astype(F32)
        for i in range(half_req):
            q = qf[:, i * heads:(i + 1) * heads, :].reshape(n_seq * heads, qf.shape[2]).astype(BF16)
            length = lengths[0, c * half_req + i]
            parts = []
            for side, base in ((0, s), (1, 2 * y + other)):
                score = lax.dot_general(
                    q, lbuf[side, i], (((1,), (0,)), ((), ())), preferred_element_type=F32
                ) * SCALE
                valid = position + base * LANE < length
                parts.append((jnp.where(valid, score, NEG), valid))
            top = jnp.maximum(
                jnp.max(parts[0][0], axis=1, keepdims=True),
                jnp.max(parts[1][0], axis=1, keepdims=True),
            ).astype(BF16).astype(F32)
            total = jnp.zeros((n_seq * heads, 1), F32)
            context = jnp.zeros((n_seq * heads, LAT), F32)
            for side in range(2):
                score, valid = parts[side]
                w = jnp.where(valid, jnp.exp(score - top), 0.0)
                total = total + jnp.sum(w, axis=1, keepdims=True)
                context = context + lax.dot_general(
                    w.astype(BF16), lbuf[side, i, 0:LAT, :], (((1,), (1,)), ((), ())),
                    preferred_element_type=F32,
                )
            total_high = total.astype(BF16).astype(F32)
            note = jnp.where(
                position == 0,
                top,
                jnp.where(position == 1, total_high, jnp.where(position == 2, total - total_high, 0.0)),
            )
            at = pl.ds(2 * heads * i, 2 * heads)
            obuf[:, at, 0:LAT] = context.astype(BF16).reshape(n_y, 2 * heads, LAT)
            obuf[:, at, LAT:LAT + LANE] = note.astype(BF16).reshape(n_y, 2 * heads, LANE)
        came = []
        for j in range(1, n_y):
            to = lax.rem(y + j, n_y)
            came.append(net.copy(obuf.at[to], orecv.at[y], (2 * to + c, e), "y"))
        orecv[y] = obuf[y]
        yield net.now + 25.0
        for one, _ in came:
            one.wait_recv()
        row = lax.broadcasted_iota(jnp.int32, fresh.shape, 0)
        all_fresh = fresh[...].astype(F32)
        own_q = qf[pl.ds(2 * y, 2)]
        for i in range(half_req):
            at = pl.ds(2 * heads * i, 2 * heads)
            key = jnp.sum(jnp.where(row == c * half_req + i, all_fresh, 0.0), axis=0, keepdims=True)
            q = own_q[:, i * heads:(i + 1) * heads, :].reshape(2 * heads, qf.shape[2])
            own = jnp.sum(q * key, axis=1, keepdims=True) * SCALE
            notes = [orecv[j, at, LAT:LAT + LANE].astype(F32) for j in range(n_y)]
            top = own
            for note in notes:
                top = jnp.maximum(top, note[:, 0:1])
            w = jnp.exp(own - top)
            total, context = w, w * key[:, 0:LAT]
            for j, note in enumerate(notes):
                w = jnp.exp(note[:, 0:1] - top)
                total = total + w * (note[:, 1:2] + note[:, 2:3])
                context = context + w * orecv[j, at, 0:LAT].astype(F32)
            context = context / total
            for core in range(2):
                cf[core, i * heads:(i + 1) * heads, :] = context[core * heads:(core + 1) * heads]
        cb[...] = cf[...].astype(BF16)
        back, when = net.copy(cb.at[other], crecv, sibling, "core")
        ctx_out[pl.ds(pl.multiple_of(c * q_rows, q_rows), q_rows), :] = cb[c]
        yield when + 5.0
        back.wait_recv()
        ctx_out[pl.ds(pl.multiple_of(other * q_rows, q_rows), q_rows), :] = crecv[...]

    attention = attend()
    next(attention)

    half_a, half_b = wide_a // 2, wide_b // 2

    def cut_a(ref, side):
        lead = (slice(None),) * (len(ref.shape) - 1)
        return ref.at[lead + (pl.ds(side * half_a, half_a),)]

    def cut_b(ref, side):
        lead = (slice(None),) * (len(ref.shape) - 1)
        size = half_b if side == 0 else ref.shape[-1] - half_b
        return ref.at[lead + (pl.ds(side * half_b, size),)]

    def nothing(at):
        return None

    def gather_a():
        yield from ring_gather(net, lambda i: xa.at[z, i], cut_a, x, NX, at_x, "x", nothing)
        yield from ring_gather(net, lambda i: xa.at[i], cut_a, z, n_z, at_z, "z", nothing)

    def gather_b():
        got = []

        def row_of(zz):
            return ring_gather(net, lambda i: xb.at[zz, i], cut_b, x, NX, at_x, "x", nothing)

        def landed(zz):
            got.append(zz)

        inner = ring_gather(net, lambda i: xb.at[i, x], cut_b, z, n_z, at_z, "z", landed)
        waiting = []
        done = False
        inner_time = None
        while True:
            if not done and (inner_time is None or not waiting or inner_time <= waiting[0][0]):
                if inner_time is not None:
                    yield inner_time
                try:
                    inner_time = next(inner)
                except StopIteration:
                    done = True
                for zz in got:
                    task = row_of(zz)
                    heapq.heappush(waiting, (next(task), len(net.copies), task))
                got.clear()
            elif waiting:
                at, _, task = heapq.heappop(waiting)
                yield at
                try:
                    heapq.heappush(waiting, (next(task), len(net.copies), task))
                except StopIteration:
                    pass
            else:
                break

    def middle():
        yield net.now + 6.0
        next(attention)

    net.run([gather_a(), gather_b(), middle()])

    for load in loads[2:]:
        load.wait()
    wg_copy.wait_recv()
    wu_copy.wait_recv()
    wd_copy.wait_recv()
    step_a, step_b = wide_a // 3, wide_b // 4
    for k in range(3):
        cols = slice(k * step_a, (k + 1) * step_a)
        term = jnp.dot(
            xa[:, :, :, cols].reshape(rows, step_a), wcat[cols, :], preferred_element_type=F32
        )
        acc[...] = term if k == 0 else acc[...] + term
    for k in range(4):
        cols = slice(k * step_b, (k + 1) * step_b)
        down = slice(wide_a + k * step_b, wide_a + (k + 1) * step_b)
        acc[...] = acc[...] + jnp.dot(
            xb[:, :, :, cols].reshape(rows, step_b), wcat[down, :], preferred_element_type=F32
        )
    tile = xb[:, :, :, wide_b:wide_b + LANE].reshape(rows, LANE).astype(F32)
    lane = lax.broadcasted_iota(jnp.int32, (rows, LANE), 1)
    gate = jnp.sum(jnp.where((lane == e) | (lane == e + experts), tile, 0.0), axis=1, keepdims=True)
    g = acc[:, 0:2 * LANE]
    hid[...] = (g / (1.0 + jnp.exp(-g)) * acc[:, 2 * LANE:4 * LANE] * gate).astype(BF16)
    for k in range(4):
        down = slice(wide_a + k * step_b, wide_a + (k + 1) * step_b)
        term = jnp.dot(hid[...], wdcat[:, down], preferred_element_type=F32)
        yb[:, :, :, k * step_b:(k + 1) * step_b] = term.astype(BF16).reshape(n_z, NX, HALF_TOK, step_b)

    net.links, net.now = {}, 0.0
    far = n_z // 2
    ahead = [far]
    for d in range(far - 1, 0, -1):
        ahead += [d, -d]
    ahead.append(0)
    ended = set()

    def row_sum(index, d):
        zz = mod(z + d, n_z)

        def finish(total):
            yb[zz, x] = total.astype(BF16)
            ended.add(d)

        return ring_scatter(
            net,
            lambda i: yb.at[zz, i],
            cut_b,
            lambda way, k: rbx.at[index, way, k],
            x, NX, at_x, "x",
            lambda d: True,
            finish,
        )

    row_tasks = [row_sum(index, d) for index, d in enumerate(ahead)]
    started = []
    for task in row_tasks:
        started.append((next(task), task))

    def resume(at, task):
        yield at
        yield from task

    for k in range(3):
        cols = slice(k * step_a, (k + 1) * step_a)
        term = jnp.dot(hid[...], wdcat[:, cols], preferred_element_type=F32)
        ya[:, :, :, cols] = term.astype(BF16).reshape(n_z, NX, HALF_TOK, step_a)

    def sum_a():
        def keep(total):
            ya[z] = total.astype(BF16)

        yield from ring_scatter(
            net, lambda i: ya.at[i], cut_a, lambda way, k: ra.at[way, k], z, n_z, at_z, "z",
            lambda d: True, keep,
        )

        def finish(total):
            line[:, 0:wide_a] = total

        yield from ring_scatter(
            net, lambda i: ya.at[z, i], cut_a, lambda way, k: rax.at[way, k], x, NX, at_x, "x",
            lambda d: True, finish,
        )

    def sum_b():
        def finish(total):
            line[:, wide_a:wide_a + wide_b] = total

        yield from ring_scatter(
            net, lambda i: yb.at[i, x], cut_b, lambda way, k: rb.at[way, k], z, n_z, at_z, "z",
            lambda d: d in ended, finish,
        )

    def rest():
        yield net.now + 4.0
        when = next(attention)
        yield when
        for _ in attention:
            pass

    net.run([sum_a()] + [resume(at, task) for at, task in started] + [sum_b(), rest()])

    for i in range(n_seq):
        begin, turn = share * i // LANE * LANE, share * i % LANE
        span = tokpad.shape[2] + LANE
        value = line[:, begin:begin + span]
        if turn:
            value = pltpu.roll(value, span - turn, 1)
        ebuf[i] = value[:, 0:tokpad.shape[2]].astype(BF16)
    each(lambda j: end_copy(j).start())
    erecv[s] = ebuf[s]
    each(lambda j: end_copy(j).wait_recv())
    for half in range(2):
        total = erecv[half].astype(F32)
        for i in range(1, n_y):
            total = total + erecv[2 * i + half].astype(F32)
        mix_out[half * HALF_TOK:(half + 1) * HALF_TOK, :] = total[:, 0:share].astype(BF16)

    each(lambda j: token_copy(j).wait_send())
    each(lambda j: query_copy(j).wait_send())
    each(lambda j: end_copy(j).wait_send())
    for made in net.copies:
        made.wait_send()


def on_device(latent, lengths, queries, fresh_latent, tokens, routes, gates, w_gate, w_up, w_down):
    n_seq, n_ep = lax.axis_size("seq"), lax.axis_size("ep")
    n_z, n_y = n_ep // NX, n_seq // 2
    n_req, heads, width = queries.shape
    share = tokens.shape[1]
    features = share * n_seq
    wide_a = features // 7 * 3
    wide_b = features - wide_a
    padded = -(-share // LANE) * LANE
    rows = n_ep * HALF_TOK
    half_req = n_req // 2
    q_rows = half_req * heads
    far_z, far_x = n_z // 2, NX // 2
    cfg = (n_seq, n_z, wide_a, wide_b, share, heads)
    vmem = pl.BlockSpec(memory_space=pltpu.VMEM)
    hbm = pl.BlockSpec(memory_space=pl.ANY)
    dma = pltpu.SemaphoreType.DMA
    ffn = 2 * rows * features * 6 * LANE
    context, mixed = pl.pallas_call(
        functools.partial(kernel, cfg),
        out_shape=(
            jax.ShapeDtypeStruct((n_req * heads, LAT), BF16),
            jax.ShapeDtypeStruct(tokens.shape, BF16),
        ),
        in_specs=[hbm, hbm, hbm, hbm, hbm, pl.BlockSpec(memory_space=pltpu.SMEM), vmem, vmem, vmem, vmem],
        out_specs=(vmem, vmem),
        scratch_shapes=[
            pltpu.VMEM((2, HALF_TOK, padded), BF16),
            pltpu.VMEM((n_seq, HALF_TOK, padded), BF16),
            pltpu.VMEM((HALF_TOK, features + 2 * LANE), F32),
            pltpu.VMEM((n_z, NX, HALF_TOK, wide_a), BF16),
            pltpu.VMEM((n_z, NX, HALF_TOK, wide_b + LANE), BF16),
            pltpu.VMEM((features, 4 * LANE), BF16),
            pltpu.VMEM((2 * LANE, features), BF16),
            pltpu.VMEM((rows, 4 * LANE), F32),
            pltpu.VMEM((rows, 2 * LANE), BF16),
            pltpu.VMEM((n_z, NX, HALF_TOK, wide_a), BF16),
            pltpu.VMEM((n_z, NX, HALF_TOK, wide_b), BF16),
            pltpu.VMEM((2, far_z, NX, HALF_TOK, wide_a), BF16),
            pltpu.VMEM((2, far_x, HALF_TOK, wide_a), BF16),
            pltpu.VMEM((n_z, 2, far_x, HALF_TOK, wide_b), BF16),
            pltpu.VMEM((2, far_z, HALF_TOK, wide_b), BF16),
            pltpu.VMEM((n_seq, HALF_TOK, padded), BF16),
            pltpu.VMEM((n_seq, HALF_TOK, padded), BF16),
            pltpu.VMEM((2, half_req, width, LANE), BF16),
            pltpu.VMEM((n_seq, q_rows, width), BF16),
            pltpu.VMEM((n_seq, q_rows, width), F32),
            pltpu.VMEM((n_y, 2 * q_rows, LAT + LANE), BF16),
            pltpu.VMEM((n_y, 2 * q_rows, LAT + LANE), BF16),
            pltpu.VMEM((2, q_rows, LAT), F32),
            pltpu.VMEM((2, q_rows, LAT), BF16),
            pltpu.VMEM((q_rows, LAT), BF16),
            dma((5,)),
            dma((140,)),
            dma((140,)),
            dma((n_seq,)),
            dma((n_seq,)),
            dma((n_seq,)),
            dma((n_seq,)),
            dma((n_seq,)),
            dma((n_seq,)),
        ],
        compiler_params=pltpu.CompilerParams(
            collective_id=0, has_side_effects=True, vmem_limit_bytes=56 * 1024 * 1024
        ),
        cost_estimate=pl.CostEstimate(flops=ffn, bytes_accessed=6 * 2**20, transcendentals=rows * 512),
    )(
        latent.transpose(0, 2, 1),
        queries.reshape(n_req * heads, width),
        w_gate[0],
        w_up[0],
        w_down[0],
        lengths,
        fresh_latent,
        tokens,
        routes,
        gates,
    )
    return context.reshape(n_req, heads, LAT), mixed


def solution(mesh):
    placed = (
        P("ep", "seq", None),
        P("ep", None),
        P("ep", "seq", None),
        P("ep", None),
        P("ep", "seq"),
        P("ep", None),
        P("ep", None),
        P("ep", None, "seq"),
        P("ep", None, "seq"),
        P("ep", "seq", None),
    )
    return jax.shard_map(
        on_device,
        mesh=mesh,
        in_specs=placed,
        out_specs=(P("ep", "seq", None), P("ep", "seq")),
        check_vma=False,
    )
```

time: 361 us -> 108 us (0.30); the launches traced: 355 us -> 107 us
  waiting for transfers between devices: 168 us -> 0 us
  Pallas kernels: 0 us -> 101 us
  local copies, waits for them, and re-layouts: 104 us -> 5.53 us
  blocking collectives: 24.7 us -> 0 us
  starting transfers between devices: 19.5 us -> 0 us
  matrix products: 17.2 us -> 0 us
  between operations: 14 us -> 0.64 us
  other arithmetic: 7.54 us -> 0 us
    pallas_call x0 -> x1, Pallas kernels: none -> 101 us  [on_device(): pl.pallas_call(functools.partial(kernel, cfg), out_shape=(jax.ShapeDtypeS...]
    all_gather x2 -> x0, waiting for transfers between devices: 85 us -> none  [the longest x1 85 us: on_device(): slot_block = lax.all_gather(arrived_rows, 'seq', axis=2, tiled=True)]
    unnamed x29 -> x4, local copies, waits for them, and re-layouts: 81.4 us -> 5.53 us
    all_to_all x3 -> x0, waiting for transfers between devices: 65.5 us -> none  [the longest x1 56.2 us: on_device(): lax.all_to_all(outgoing, 'seq', split_axis=0, concat_axis=0, tiled=True)]
    all_to_all x1 -> x0, blocking collectives: 24.7 us -> none  [on_device(): lax.all_to_all(placed.reshape(ep_count, local_experts * capacity, -1), 'e...]
    all_to_all x3 -> x0, starting transfers between devices: 19.4 us -> none  [the longest x1 9.9 us: on_device(): lax.all_to_all(block_sums, 'ep', split_axis=0, concat_axis=0, tiled=True)]
    unnamed x4 -> x0, waiting for transfers between devices: 17.8 us -> none
    all_gather x1 -> x0, local copies, waits for them, and re-layouts: 17.5 us -> none  [on_device(): slot_block = lax.all_gather(arrived_rows, 'seq', axis=2, tiled=True)]
  transfers between devices with their start and end apart: 6 -> 0, of which waited for: 4 -> 0; matrix products, arithmetic and copies ran while one was open for 34% -> 0% of each run, Pallas kernels for 0% -> 0%
where the time goes in v1:
time: 108 us; the launch traced here: 107 us
  Pallas kernels  101 us (94%)
  local copies, waits for them, and re-layouts  5.53 us (5%)
    pallas_call x1, Pallas kernels, on_device(): pl.pallas_call(functools.partial(kernel, cfg), out_shape=(jax.ShapeDtypeS...  101 us
    unnamed x4, local copies, waits for them, and re-layouts  5.53 us

profile of v1, /device:TPU:1, one launch (start us, length us, event | category | flops | bytes accessed | tf_op | source)
XLA Modules:
  0.0 107.2 jit_solution(14151144303145669612)
XLA Ops:
  0.6 1.4 %copy.12.routes = s32[32,8]{1,0:T(8,128)} copy(s32[32,8]{0,1:T(8,128)} %param.15) | data formatting | bytes 2048 | tf_op args[5]
  2.0 1.4 %copy.13.gates = f32[32,8]{1,0:T(8,128)} copy(f32[32,8]{0,1:T(8,128)} %param.16) | data formatting | bytes 2048 | tf_op args[6]
  3.4 101.0 %shard_map.113 = (bf16[64,512]{1,0:T(8,128)(2,1)}, bf16[32,224]{1,0:T(8,128)(2,1)}) custom-call(bf16[8,576,128]{2,1,0:T(8,128)(2,1)} %bitcast.7, bf16[64,576]{1,0:T(8,128)(2,1)} %bitcast.11, bf16[3584,128]{1,0:T(8,128)(2,1)} %bitcast.8, bf16[3584,128]{1,0:T(8,128)(2,1)} %bitcast.9, bf16[128,3584]{1,0:T(8,128)(2,1)} %bitcast.10, s32[1,8]{1,0:T(1,128)} %lengths.1, ...), custom_call_target="tpu_custom_call" | custom-call | flops 2818572288 | bytes 6291456 | tf_op jit(solution)/shard_map/pallas_call | solution.py:572
  104.4 1.5 %copy.16 = bf16[8,8,512]{2,1,0:T(8,128)(2,1)} copy(bf16[8,8,512]{2,1,0:T(8,128)(2,1)} %bitcast.6) | data formatting | bytes 131072
  105.9 1.3 %copy.17 = bf16[32,224]{1,0:T(8,128)(2,1)} copy(bf16[32,224]{1,0:T(8,128)(2,1)} %get-tuple-element.9) | data formatting | bytes 28672

commit v2 on v1

v2 whole, which is shorter than its diff:
```python
import functools
import heapq

import jax
import jax.numpy as jnp
from jax import lax
from jax.experimental import pallas as pl
from jax.experimental.pallas import tpu as pltpu
from jax.sharding import PartitionSpec as P

MESH = pl.DeviceIdType.MESH
LAT = 512
NX = 4
LANE = 128
HALF_TOK = 16
SCALE = 0.07216878364870322
NEG = -1.0e30
F32 = jnp.float32
BF16 = jnp.bfloat16

LINK_RATE = 45.0e3
HOP = 1.5


def mod(value, n):
    return lax.rem(value + n, n)


class Net:
    def __init__(self, send, recv):
        self.send, self.recv = send, recv
        self.count, self.now = 0, 0.0
        self.links, self.copies = {}, []

    def copy(self, src, dst, device, link):
        at = self.count
        self.count += 1
        made = pltpu.make_async_remote_copy(
            src_ref=src,
            dst_ref=dst,
            send_sem=self.send.at[at],
            recv_sem=self.recv.at[at],
            device_id=device,
            device_id_type=MESH,
        )
        made.start()
        size = 2
        for extent in src.shape:
            size *= extent
        begin = max(self.links.get(link, 0.0), self.now)
        self.links[link] = begin + size / LINK_RATE
        self.copies.append(made)
        return made, self.links[link] + HOP

    def run(self, tasks):
        self.heap, self.order = [], 0
        for task in tasks:
            self.add(self.now, task)
        while self.heap:
            at, _, task = heapq.heappop(self.heap)
            self.now = max(self.now, at)
            try:
                ready = next(task)
            except StopIteration:
                continue
            self.add(ready, task)

    def add(self, at, task):
        self.order += 1
        heapq.heappush(self.heap, (at, self.order, task))


def around(n):
    offsets = [0]
    for k in range(1, n // 2):
        offsets += [k, -k]
    return offsets + [n // 2]


def ring_gather(net, piece, cut, n, up, down, axis, landed):
    far = n // 2

    def pass_on(side, k):
        src, dst = piece((k, -k)[1 - side]), piece(far if k + 1 == far else (k + 1, -k - 1)[1 - side])
        if k + 1 == far:
            src, dst = cut(src, side), cut(dst, side)
        return net.copy(src, dst, (up, down)[side], axis + "+-"[side])

    cu, tu = pass_on(0, 0)
    cd, td = pass_on(1, 0)
    landed(0)
    for k in range(1, far):
        yield tu
        cu.wait_recv()
        cu, tu = pass_on(0, k)
        landed(-k)
        yield td
        cd.wait_recv()
        cd, td = pass_on(1, k)
        landed(k)
    yield max(tu, td)
    cu.wait_recv()
    cd.wait_recv()
    landed(far)


def add_into(ref, other):
    ref[...] = ref[...] + other[...]


def ring_scatter(net, piece, cut, arrived, n, up, down, axis, ready, finish):
    far = n // 2
    while not ready(far):
        yield net.now + 0.01
    cu, tu = net.copy(cut(piece(far), 0), cut(arrived(0, 0), 0), up, axis + "+")
    cd, td = net.copy(cut(piece(far), 1), cut(arrived(1, 0), 1), down, axis + "-")
    for k in range(1, far):
        d = far - k
        while not (ready(d) and ready(-d)):
            yield net.now + 0.01
        yield tu
        cu.wait_recv()
        mine, came = piece(d), arrived(0, k - 1)
        if k == 1:
            mine, came = cut(mine, 0), cut(came, 0)
        add_into(mine, came)
        cu, tu = net.copy(piece(d), arrived(0, k), up, axis + "+")
        yield td
        cd.wait_recv()
        mine, came = piece(-d), arrived(1, k - 1)
        if k == 1:
            mine, came = cut(mine, 1), cut(came, 1)
        add_into(mine, came)
        cd, td = net.copy(piece(-d), arrived(1, k), down, axis + "-")
    while not ready(0):
        yield net.now + 0.01
    yield max(tu, td)
    cu.wait_recv()
    cd.wait_recv()
    if far == 1:
        add_into(cut(piece(0), 0), cut(arrived(0, 0), 0))
        add_into(cut(piece(0), 1), cut(arrived(1, 0), 1))
        finish(piece(0)[...].astype(F32))
    else:
        finish(
            piece(0)[...].astype(F32)
            + arrived(0, far - 1)[...].astype(F32)
            + arrived(1, far - 1)[...].astype(F32)
        )


def kernel(
    cfg,
    latent, queries, wg, wu, wd, lengths, fresh, tokens, routes, gates,
    ctx_out, mix_out,
    tokpad, tokbuf, line, square, xa, xb, wcat, wdcat, acc, hid, ya, yb,
    ra, rax, rbx, rb, ebuf, erecv,
    lbuf, qbuf, qf, obuf, orecv, cf, cb, crecv,
    local_sem, send_sem, recv_sem, t_send, t_recv, q_send, q_recv, e_send, e_recv,
):
    n_seq, n_z, wide_a, wide_b, share, heads = cfg
    n_y = n_seq // 2
    s, e = lax.axis_index("seq"), lax.axis_index("ep")
    y, c = s // 2, lax.rem(s, 2)
    z, x = e // NX, lax.rem(e, NX)
    other = 1 - c
    sibling = (2 * y + other, e)
    experts = n_z * NX
    n_req = lengths.shape[1]
    half_req = n_req // 2
    q_rows = half_req * heads
    x_up, x_down = (s, z * NX + mod(x + 1, NX)), (s, z * NX + mod(x - 1, NX))
    z_up, z_down = (s, mod(z + 1, n_z) * NX + x), (s, mod(z - 1, n_z) * NX + x)
    slot_z = {d: i for i, d in enumerate(around(n_z))}
    slot_x = {d: i for i, d in enumerate(around(NX))}

    def local(src, dst, i):
        made = pltpu.make_async_copy(src, dst, local_sem.at[i])
        made.start()
        return made

    for half in range(2):
        tokpad[half] = jnp.zeros_like(tokpad[half])
        tokpad[half, :, 0:share] = tokens[half * HALF_TOK:(half + 1) * HALF_TOK, :]

    barrier = pltpu.get_barrier_semaphore()

    def greet(j, carry):
        pl.semaphore_signal(
            barrier, inc=1, device_id=(lax.rem(s + j, n_seq), e), device_id_type=MESH
        )
        return carry

    lax.fori_loop(1, n_seq, greet, 0)
    for who in (x_up, x_down, z_up, z_down):
        pl.semaphore_signal(barrier, inc=1, device_id=who, device_id_type=MESH)

    mine_q = queries.at[pl.ds(pl.multiple_of(c * q_rows, q_rows), q_rows)]
    loads = [
        local(mine_q, qbuf.at[s], 0),
        local(latent.at[pl.ds(c * half_req, half_req)], lbuf.at[0], 1),
        local(wg, wcat.at[:, pl.ds(0, LANE)], 2),
        local(wu, wcat.at[:, pl.ds(2 * LANE, LANE)], 3),
        local(wd, wdcat.at[pl.ds(0, LANE)], 4),
    ]

    row = lax.broadcasted_iota(jnp.int32, (LANE, routes.shape[1]), 0)
    named = jnp.where(row < experts, row, row - experts)
    weight = jnp.zeros(named.shape, F32)
    for k in range(routes.shape[0]):
        weight = weight + jnp.where(named == routes[k:k + 1, :], gates[k:k + 1, :], 0.0)
    high = weight.astype(BF16).astype(F32)
    weight = jnp.where(row < experts, high, jnp.where(row < 2 * experts, weight - high, 0.0))
    square[...] = jnp.zeros_like(square)
    square[:, 0:routes.shape[1]] = weight
    square[...] = jnp.transpose(square[...])

    pl.semaphore_wait(barrier, n_seq - 1 + 4)

    def token_copy(j):
        to = lax.rem(s + j, n_seq)
        return pltpu.make_async_remote_copy(
            src_ref=tokpad.at[lax.rem(to, 2)],
            dst_ref=tokbuf.at[s],
            send_sem=t_send.at[j],
            recv_sem=t_recv.at[j],
            device_id=(to, e),
            device_id_type=MESH,
        )

    def query_copy(j):
        to = lax.rem(s + j, n_seq)
        begin = pl.multiple_of(lax.rem(to, 2) * q_rows, q_rows)
        return pltpu.make_async_remote_copy(
            src_ref=queries.at[pl.ds(begin, q_rows)],
            dst_ref=qbuf.at[s],
            send_sem=q_send.at[j],
            recv_sem=q_recv.at[j],
            device_id=(to, e),
            device_id_type=MESH,
        )

    def end_copy(j):
        to = lax.rem(s + j, n_seq)
        return pltpu.make_async_remote_copy(
            src_ref=ebuf.at[to],
            dst_ref=erecv.at[s],
            send_sem=e_send.at[j],
            recv_sem=e_recv.at[j],
            device_id=(to, e),
            device_id_type=MESH,
        )

    def each(act):
        def body(j, carry):
            act(j)
            return carry

        lax.fori_loop(1, n_seq, body, 0)

    net = Net(send_sem, recv_sem)
    each(lambda j: token_copy(j).start())
    each(lambda j: query_copy(j).start())
    lat_copy, _ = net.copy(latent.at[pl.ds(other * half_req, half_req)], lbuf.at[1], sibling, "core")

    tokbuf[s] = tokpad[c]
    line[...] = jnp.zeros_like(line)
    first_row = pl.multiple_of(c * HALF_TOK, HALF_TOK)
    xb[0, 0, :, wide_b:wide_b + LANE] = square[pl.ds(first_row, HALF_TOK), :].astype(BF16)
    each(lambda j: token_copy(j).wait_recv())
    for i in range(n_seq):
        begin, turn = share * i // LANE * LANE, share * i % LANE
        span = tokpad.shape[2] + LANE
        value = jnp.concatenate(
            [tokbuf[i].astype(F32), jnp.zeros((HALF_TOK, LANE), F32)], axis=1
        )
        if turn:
            value = pltpu.roll(value, turn, 1)
        line[:, begin:begin + span] = line[:, begin:begin + span] + value
    xa[0, 0] = line[:, 0:wide_a].astype(BF16)
    xb[0, 0, :, 0:wide_b] = line[:, wide_a:wide_a + wide_b].astype(BF16)

    position = lax.broadcasted_iota(jnp.int32, (n_seq * heads, LANE), 1)

    def one_request(i, carry):
        head_rows = pl.ds(pl.multiple_of(i * heads, heads), heads)
        q = qf[:, head_rows, :].reshape(n_seq * heads, qf.shape[2]).astype(BF16)
        length = lengths[0, c * half_req + i]
        parts = []
        for side, base in ((0, s), (1, 2 * y + other)):
            score = jnp.dot(q, lbuf[side, i], preferred_element_type=F32) * SCALE
            valid = position + base * LANE < length
            parts.append((jnp.where(valid, score, NEG), valid))
        top = jnp.maximum(
            jnp.max(parts[0][0], axis=1, keepdims=True),
            jnp.max(parts[1][0], axis=1, keepdims=True),
        ).astype(BF16).astype(F32)
        total = jnp.zeros((n_seq * heads, 1), F32)
        context = jnp.zeros((n_seq * heads, LAT), F32)
        for side in range(2):
            score, valid = parts[side]
            w = jnp.where(valid, jnp.exp(score - top), 0.0)
            total = total + jnp.sum(w, axis=1, keepdims=True)
            context = context + lax.dot_general(
                w.astype(BF16), lbuf[side, i, 0:LAT, :], (((1,), (1,)), ((), ())),
                preferred_element_type=F32,
            )
        total_high = total.astype(BF16).astype(F32)
        note = jnp.where(
            position == 0,
            top,
            jnp.where(position == 1, total_high, jnp.where(position == 2, total - total_high, 0.0)),
        )
        at = pl.ds(pl.multiple_of(2 * heads * i, 2 * heads), 2 * heads)
        obuf[:, at, 0:LAT] = context.astype(BF16).reshape(n_y, 2 * heads, LAT)
        obuf[:, at, LAT:LAT + LANE] = note.astype(BF16).reshape(n_y, 2 * heads, LANE)
        return carry

    def one_context(i, carry):
        at = pl.ds(pl.multiple_of(2 * heads * i, 2 * heads), 2 * heads)
        head_rows = pl.ds(pl.multiple_of(i * heads, heads), heads)
        line_of = lax.broadcasted_iota(jnp.int32, fresh.shape, 0)
        chosen = jnp.where(line_of == c * half_req + i, fresh[...].astype(F32), 0.0)
        key = jnp.sum(chosen, axis=0, keepdims=True)
        q = qf[pl.ds(2 * y, 2), head_rows, :].reshape(2 * heads, qf.shape[2])
        own = jnp.sum(q * key, axis=1, keepdims=True) * SCALE
        notes = [orecv[j, at, LAT:LAT + LANE].astype(F32) for j in range(n_y)]
        top = own
        for note in notes:
            top = jnp.maximum(top, note[:, 0:1])
        w = jnp.exp(own - top)
        total, context = w, w * key[:, 0:LAT]
        for j, note in enumerate(notes):
            w = jnp.exp(note[:, 0:1] - top)
            total = total + w * (note[:, 1:2] + note[:, 2:3])
            context = context + w * orecv[j, at, 0:LAT].astype(F32)
        context = context / total
        for core in range(2):
            cf[core, head_rows, :] = context[core * heads:(core + 1) * heads]
        return carry

    def attend():
        yield net.now + 8.0
        loads[0].wait()
        loads[1].wait()
        each(lambda j: query_copy(j).wait_recv())
        lat_copy.wait_recv()
        qf[...] = qbuf[...].astype(F32)
        lax.fori_loop(0, half_req // 2, one_request, 0)
        net.now += 2.0
        yield net.now + 0.5
        lax.fori_loop(half_req // 2, half_req, one_request, 0)
        net.now += 2.0
        came = []
        for j in range(1, n_y):
            to = lax.rem(y + j, n_y)
            came.append(net.copy(obuf.at[to], orecv.at[y], (2 * to + c, e), "y"))
        orecv[y] = obuf[y]
        yield net.now + 25.0
        for one, _ in came:
            one.wait_recv()
        lax.fori_loop(0, half_req, one_context, 0)
        net.now += 1.0
        cb[...] = cf[...].astype(BF16)
        back, when = net.copy(cb.at[other], crecv, sibling, "core")
        ctx_out[pl.ds(pl.multiple_of(c * q_rows, q_rows), q_rows), :] = cb[c]
        yield when + 5.0
        back.wait_recv()
        ctx_out[pl.ds(pl.multiple_of(other * q_rows, q_rows), q_rows), :] = crecv[...]

    half_a, half_b = wide_a // 2, wide_b // 2

    def cut_a(ref, side):
        return ref.at[:, pl.ds(side * half_a, half_a)]

    def cut_b(ref, side):
        return ref.at[:, pl.ds(side * half_b, half_b if side == 0 else ref.shape[-1] - half_b)]

    landed = {d: 0 for d in slot_z}

    def count(d):
        landed[d] += 1

    def gather_a():
        def start(dx):
            at = slot_x[dx]
            net.add(net.now, ring_gather(
                net, lambda d: xa.at[slot_z[d], at], cut_a, n_z, z_up, z_down, "z", count
            ))

        yield from ring_gather(
            net, lambda d: xa.at[0, slot_x[d]], cut_a, NX, x_up, x_down, "x", start
        )

    def gather_b():
        def start(dz):
            at = slot_z[dz]
            net.add(net.now, ring_gather(
                net, lambda d: xb.at[at, slot_x[d]], cut_b, NX, x_up, x_down, "x", lambda d: count(dz)
            ))

        yield from ring_gather(
            net, lambda d: xb.at[slot_z[d], 0], cut_b, n_z, z_up, z_down, "z", start
        )

    step_a, step_b = wide_a // 3, wide_b // 4
    weights = []

    def load_weights():
        yield net.now + 0.5
        for src, dst in (
            (wg, wcat.at[:, pl.ds(LANE, LANE)]),
            (wu, wcat.at[:, pl.ds(3 * LANE, LANE)]),
            (wd, wdcat.at[pl.ds(LANE, LANE)]),
        ):
            weights.append(net.copy(src, dst, sibling, "core")[0])

    def experts_of(first, last):
        rows = (last - first) * NX * HALF_TOK

        def up_a(k, carry):
            cols = pl.ds(pl.multiple_of(k * step_a, step_a), step_a)
            value = xa[first:last, :, :, cols].reshape(rows, step_a)
            acc[0:rows, :] += jnp.dot(value, wcat[cols, :], preferred_element_type=F32)
            return carry

        def up_b(k, carry):
            cols = pl.ds(pl.multiple_of(k * step_b, step_b), step_b)
            down = pl.ds(pl.multiple_of(wide_a + k * step_b, step_b), step_b)
            value = xb[first:last, :, :, cols].reshape(rows, step_b)
            acc[0:rows, :] += jnp.dot(value, wcat[down, :], preferred_element_type=F32)
            return carry

        def down_a(k, carry):
            cols = pl.ds(pl.multiple_of(k * step_a, step_a), step_a)
            value = jnp.dot(hid[0:rows, :], wdcat[:, cols], preferred_element_type=F32)
            ya[first:last, :, :, cols] = value.astype(BF16).reshape(last - first, NX, HALF_TOK, step_a)
            return carry

        def down_b(k, carry):
            cols = pl.ds(pl.multiple_of(k * step_b, step_b), step_b)
            down = pl.ds(pl.multiple_of(wide_a + k * step_b, step_b), step_b)
            value = jnp.dot(hid[0:rows, :], wdcat[:, down], preferred_element_type=F32)
            yb[first:last, :, :, cols] = value.astype(BF16).reshape(last - first, NX, HALF_TOK, step_b)
            return carry

        acc[0:rows, :] = jnp.zeros((rows, 4 * LANE), F32)
        lax.fori_loop(0, 3, up_a, 0)
        lax.fori_loop(0, 4, up_b, 0)
        tile = xb[first:last, :, :, wide_b:wide_b + LANE].reshape(rows, LANE).astype(F32)
        lane = lax.broadcasted_iota(jnp.int32, (rows, LANE), 1)
        gate = jnp.sum(
            jnp.where((lane == e) | (lane == e + experts), tile, 0.0), axis=1, keepdims=True
        )
        g = acc[0:rows, 0:2 * LANE]
        value = g / (1.0 + jnp.exp(-g)) * acc[0:rows, 2 * LANE:4 * LANE] * gate
        hid[0:rows, :] = value.astype(BF16)
        lax.fori_loop(0, 4, down_b, 0)
        lax.fori_loop(0, 3, down_a, 0)

    def compute():
        offsets = around(n_z)
        groups = [(0, 3), (3, 5), (5, 7), (7, 8)] if n_z == 8 else [(0, len(offsets))]
        for first, last in groups:
            while any(landed[d] < 2 * NX for d in offsets[first:last]):
                yield net.now + 0.01
            if first == 0:
                for load in loads[2:]:
                    load.wait()
                for made in weights:
                    made.wait_recv()
            experts_of(first, last)
            net.now += 1.0

    attention = attend()
    net.run([gather_a(), gather_b(), load_weights(), sample(attention, 3), compute()])

    net.links, net.now = {}, 0.0
    ended = set()

    def always(d):
        return True

    def row_sum(dz):
        at = slot_z[dz]

        def finish(total):
            yb[at, 0] = total.astype(BF16)
            ended.add(dz)

        return ring_scatter(
            net, lambda d: yb.at[at, slot_x[d]], cut_b, lambda way, k: rbx.at[at, way, k],
            NX, x_up, x_down, "x", always, finish,
        )

    done_a = set()

    def column_sum(dx):
        at = slot_x[dx]

        def finish(total):
            ya[0, at] = total.astype(BF16)
            done_a.add(dx)

        return ring_scatter(
            net, lambda d: ya.at[slot_z[d], at], cut_a, lambda way, k: ra.at[at, way, k],
            n_z, z_up, z_down, "z", always, finish,
        )

    def end_a(total):
        line[:, 0:wide_a] = total

    def end_b(total):
        line[:, wide_a:wide_a + wide_b] = total

    sum_a = ring_scatter(
        net, lambda d: ya.at[0, slot_x[d]], cut_a, lambda way, k: rax.at[way, k],
        NX, x_up, x_down, "x", lambda d: d in done_a, end_a,
    )
    sum_b = ring_scatter(
        net, lambda d: yb.at[slot_z[d], 0], cut_b, lambda way, k: rb.at[way, k],
        n_z, z_up, z_down, "z", lambda d: d in ended, end_b,
    )
    rows_first = [row_sum(d) for d in reversed(around(n_z))]
    columns_first = [column_sum(d) for d in reversed(around(NX))]
    mixed = []
    while rows_first or columns_first:
        if rows_first:
            mixed.append(rows_first.pop(0))
        if columns_first:
            mixed.append(columns_first.pop(0))
    net.run(mixed + [sum_a, sum_b, sample(attention, 9)])

    for i in range(n_seq):
        begin, turn = share * i // LANE * LANE, share * i % LANE
        span = tokpad.shape[2] + LANE
        value = line[:, begin:begin + span]
        if turn:
            value = pltpu.roll(value, span - turn, 1)
        ebuf[i] = value[:, 0:tokpad.shape[2]].astype(BF16)
    each(lambda j: end_copy(j).start())
    erecv[s] = ebuf[s]
    each(lambda j: end_copy(j).wait_recv())
    for half in range(2):
        total = erecv[half].astype(F32)
        for i in range(1, n_y):
            total = total + erecv[2 * i + half].astype(F32)
        mix_out[half * HALF_TOK:(half + 1) * HALF_TOK, :] = total[:, 0:share].astype(BF16)

    each(lambda j: token_copy(j).wait_send())
    each(lambda j: query_copy(j).wait_send())
    each(lambda j: end_copy(j).wait_send())
    for made in net.copies:
        made.wait_send()


def sample(task, most):
    for _ in range(most):
        try:
            ready = next(task)
        except StopIteration:
            return
        yield ready


def on_device(latent, lengths, queries, fresh_latent, tokens, routes, gates, w_gate, w_up, w_down):
    n_seq, n_ep = lax.axis_size("seq"), lax.axis_size("ep")
    n_z, n_y = n_ep // NX, n_seq // 2
    n_req, heads, width = queries.shape
    share = tokens.shape[1]
    features = share * n_seq
    wide_a = features // 7 * 3
    wide_b = features - wide_a
    padded = -(-share // LANE) * LANE
    rows = n_ep * HALF_TOK
    half_req = n_req // 2
    q_rows = half_req * heads
    far_z, far_x = n_z // 2, NX // 2
    cfg = (n_seq, n_z, wide_a, wide_b, share, heads)
    vmem = pl.BlockSpec(memory_space=pltpu.VMEM)
    hbm = pl.BlockSpec(memory_space=pl.ANY)
    dma = pltpu.SemaphoreType.DMA
    ffn = 2 * rows * features * 6 * LANE
    context, mixed = pl.pallas_call(
        functools.partial(kernel, cfg),
        out_shape=(
            jax.ShapeDtypeStruct((n_req * heads, LAT), BF16),
            jax.ShapeDtypeStruct(tokens.shape, BF16),
        ),
        in_specs=[hbm, hbm, hbm, hbm, hbm, pl.BlockSpec(memory_space=pltpu.SMEM), vmem, vmem, vmem, vmem],
        out_specs=(vmem, vmem),
        scratch_shapes=[
            pltpu.VMEM((2, HALF_TOK, padded), BF16),
            pltpu.VMEM((n_seq, HALF_TOK, padded), BF16),
            pltpu.VMEM((HALF_TOK, features + 2 * LANE), F32),
            pltpu.VMEM((LANE, LANE), F32),
            pltpu.VMEM((n_z, NX, HALF_TOK, wide_a), BF16),
            pltpu.VMEM((n_z, NX, HALF_TOK, wide_b + LANE), BF16),
            pltpu.VMEM((features, 4 * LANE), BF16),
            pltpu.VMEM((2 * LANE, features), BF16),
            pltpu.VMEM((rows, 4 * LANE), F32),
            pltpu.VMEM((rows, 2 * LANE), BF16),
            pltpu.VMEM((n_z, NX, HALF_TOK, wide_a), BF16),
            pltpu.VMEM((n_z, NX, HALF_TOK, wide_b), BF16),
            pltpu.VMEM((NX, 2, far_z, HALF_TOK, wide_a), BF16),
            pltpu.VMEM((2, far_x, HALF_TOK, wide_a), BF16),
            pltpu.VMEM((n_z, 2, far_x, HALF_TOK, wide_b), BF16),
            pltpu.VMEM((2, far_z, HALF_TOK, wide_b), BF16),
            pltpu.VMEM((n_seq, HALF_TOK, padded), BF16),
            pltpu.VMEM((n_seq, HALF_TOK, padded), BF16),
            pltpu.VMEM((2, half_req, width, LANE), BF16),
            pltpu.VMEM((n_seq, q_rows, width), BF16),
            pltpu.VMEM((n_seq, q_rows, width), F32),
            pltpu.VMEM((n_y, 2 * q_rows, LAT + LANE), BF16),
            pltpu.VMEM((n_y, 2 * q_rows, LAT + LANE), BF16),
            pltpu.VMEM((2, q_rows, LAT), F32),
            pltpu.VMEM((2, q_rows, LAT), BF16),
            pltpu.VMEM((q_rows, LAT), BF16),
            dma((5,)),
            dma((200,)),
            dma((200,)),
            dma((n_seq,)),
            dma((n_seq,)),
            dma((n_seq,)),
            dma((n_seq,)),
            dma((n_seq,)),
            dma((n_seq,)),
        ],
        compiler_params=pltpu.CompilerParams(
            collective_id=0, has_side_effects=True, vmem_limit_bytes=56 * 1024 * 1024
        ),
        cost_estimate=pl.CostEstimate(flops=ffn, bytes_accessed=6 * 2**20, transcendentals=rows * 512),
    )(
        latent.transpose(0, 2, 1),
        queries.reshape(n_req * heads, width),
        w_gate[0],
        w_up[0],
        w_down[0],
        lengths,
        fresh_latent,
        tokens,
        routes.T,
        gates.T,
    )
    return context.reshape(n_req, heads, LAT), mixed


def solution(mesh):
    placed = (
        P("ep", "seq", None),
        P("ep", None),
        P("ep", "seq", None),
        P("ep", None),
        P("ep", "seq"),
        P("ep", None),
        P("ep", None),
        P("ep", None, "seq"),
        P("ep", None, "seq"),
        P("ep", "seq", None),
    )
    return jax.shard_map(
        on_device,
        mesh=mesh,
        in_specs=placed,
        out_specs=(P("ep", "seq", None), P("ep", "seq")),
        check_vma=False,
    )
```

time: 108 us -> 104 us (0.963)
  local copies, waits for them, and re-layouts: 5.53 us -> 2.8 us
    unnamed x4 -> x2, local copies, waits for them, and re-layouts: 5.53 us -> 2.8 us
where the time goes in v2:
time: 104 us
  Pallas kernels  101 us (97%)
  local copies, waits for them, and re-layouts  2.8 us (3%)
    pallas_call x1, Pallas kernels, on_device(): pl.pallas_call(functools.partial(kernel, cfg), out_shape=(jax.ShapeDtypeS...  101 us
    unnamed x2, local copies, waits for them, and re-layouts  2.8 us

profile of v2, /device:TPU:1, one launch (start us, length us, event | category | flops | bytes accessed | tf_op | source)
XLA Modules:
  0.0 104.0 jit_solution(4417351784708928300)
XLA Ops:
  0.6 100.6 %shard_map.113 = (bf16[64,512]{1,0:T(8,128)(2,1)}, bf16[32,224]{1,0:T(8,128)(2,1)}) custom-call(bf16[8,576,128]{2,1,0:T(8,128)(2,1)} %bitcast.9, bf16[64,576]{1,0:T(8,128)(2,1)} %bitcast.13, bf16[3584,128]{1,0:T(8,128)(2,1)} %bitcast.10, bf16[3584,128]{1,0:T(8,128)(2,1)} %bitcast.11, bf16[128,3584]{1,0:T(8,128)(2,1)} %bitcast.12, s32[1,8]{1,0:T(1,128)} %lengths.1, ...), custom_call_target="tpu_custom_call" | custom-call | flops 2818572288 | bytes 6291456 | tf_op jit(solution)/shard_map/pallas_call | solution.py:584
  101.2 1.5 %copy.14 = bf16[8,8,512]{2,1,0:T(8,128)(2,1)} copy(bf16[8,8,512]{2,1,0:T(8,128)(2,1)} %bitcast.8) | data formatting | bytes 131072
  102.7 1.3 %copy.15 = bf16[32,224]{1,0:T(8,128)(2,1)} copy(bf16[32,224]{1,0:T(8,128)(2,1)} %get-tuple-element.9) | data formatting | bytes 28672

commit v3 on v2

--- a/solution.py
+++ b/solution.py
@@ -371,33 +371,44 @@
     half_a, half_b = wide_a // 2, wide_b // 2
 
     def cut_a(ref, side):
-        return ref.at[:, pl.ds(side * half_a, half_a)]
+        lead = (slice(None),) * (len(ref.shape) - 1)
+        return ref.at[lead + (pl.ds(side * half_a, half_a),)]
 
     def cut_b(ref, side):
-        return ref.at[:, pl.ds(side * half_b, half_b if side == 0 else ref.shape[-1] - half_b)]
+        lead = (slice(None),) * (len(ref.shape) - 1)
+        size = half_b if side == 0 else ref.shape[-1] - half_b
+        return ref.at[lead + (pl.ds(side * half_b, size),)]
+
+    teams = [(0,)] + [(d, -d) for d in range(1, n_z // 2)] + [(n_z // 2,)]
+
+    def slots(team):
+        return pl.ds(slot_z[team[0]], len(team))
 
     landed = {d: 0 for d in slot_z}
 
-    def count(d):
-        landed[d] += 1
+    def count(team):
+        for d in team:
+            landed[d] += 1
 
     def gather_a():
-        def start(dx):
-            at = slot_x[dx]
-            net.add(net.now, ring_gather(
-                net, lambda d: xa.at[slot_z[d], at], cut_a, n_z, z_up, z_down, "z", count
-            ))
-
         yield from ring_gather(
-            net, lambda d: xa.at[0, slot_x[d]], cut_a, NX, x_up, x_down, "x", start
+            net, lambda d: xa.at[0, slot_x[d]], cut_a, NX, x_up, x_down, "x", lambda d: None
+        )
+        yield from ring_gather(
+            net, lambda d: xa.at[slot_z[d]], cut_a, n_z, z_up, z_down, "z", lambda d: count((d,))
         )
 
     def gather_b():
+        here = set()
+
         def start(dz):
-            at = slot_z[dz]
-            net.add(net.now, ring_gather(
-                net, lambda d: xb.at[at, slot_x[d]], cut_b, NX, x_up, x_down, "x", lambda d: count(dz)
-            ))
+            here.add(dz)
+            team = [team for team in teams if dz in team][0]
+            if here.issuperset(team):
+                net.add(net.now, ring_gather(
+                    net, lambda d: xb.at[slots(team), slot_x[d]], cut_b, NX, x_up, x_down, "x",
+                    lambda d: count(team),
+                ))
 
         yield from ring_gather(
             net, lambda d: xb.at[slot_z[d], 0], cut_b, n_z, z_up, z_down, "z", start
@@ -462,7 +473,7 @@
         offsets = around(n_z)
         groups = [(0, 3), (3, 5), (5, 7), (7, 8)] if n_z == 8 else [(0, len(offsets))]
         for first, last in groups:
-            while any(landed[d] < 2 * NX for d in offsets[first:last]):
+            while any(landed[d] < 1 + NX for d in offsets[first:last]):
                 yield net.now + 0.01
             if first == 0:
                 for load in loads[2:]:
@@ -481,31 +492,20 @@
     def always(d):
         return True
 
-    def row_sum(dz):
-        at = slot_z[dz]
+    def row_sum(team):
+        at = slots(team)
 
         def finish(total):
             yb[at, 0] = total.astype(BF16)
-            ended.add(dz)
+            ended.update(team)
 
         return ring_scatter(
-            net, lambda d: yb.at[at, slot_x[d]], cut_b, lambda way, k: rbx.at[at, way, k],
+            net, lambda d: yb.at[at, slot_x[d]], cut_b, lambda way, k: rbx.at[way, k, at],
             NX, x_up, x_down, "x", always, finish,
         )
 
-    done_a = set()
-
-    def column_sum(dx):
-        at = slot_x[dx]
-
-        def finish(total):
-            ya[0, at] = total.astype(BF16)
-            done_a.add(dx)
-
-        return ring_scatter(
-            net, lambda d: ya.at[slot_z[d], at], cut_a, lambda way, k: ra.at[at, way, k],
-            n_z, z_up, z_down, "z", always, finish,
-        )
+    def keep_a(total):
+        ya[0] = total.astype(BF16)
 
     def end_a(total):
         line[:, 0:wide_a] = total
@@ -513,23 +513,31 @@
     def end_b(total):
         line[:, wide_a:wide_a + wide_b] = total
 
-    sum_a = ring_scatter(
-        net, lambda d: ya.at[0, slot_x[d]], cut_a, lambda way, k: rax.at[way, k],
-        NX, x_up, x_down, "x", lambda d: d in done_a, end_a,
-    )
+    def sum_a():
+        yield from ring_scatter(
+            net, lambda d: ya.at[slot_z[d]], cut_a, lambda way, k: ra.at[way, k],
+            n_z, z_up, z_down, "z", always, keep_a,
+        )
+        yield from ring_scatter(
+            net, lambda d: ya.at[0, slot_x[d]], cut_a, lambda way, k: rax.at[way, k],
+            NX, x_up, x_down, "x", always, end_a,
+        )
+
     sum_b = ring_scatter(
         net, lambda d: yb.at[slot_z[d], 0], cut_b, lambda way, k: rb.at[way, k],
         n_z, z_up, z_down, "z", lambda d: d in ended, end_b,
     )
-    rows_first = [row_sum(d) for d in reversed(around(n_z))]
-    columns_first = [column_sum(d) for d in reversed(around(NX))]
-    mixed = []
-    while rows_first or columns_first:
-        if rows_first:
-            mixed.append(rows_first.pop(0))
-        if columns_first:
-            mixed.append(columns_first.pop(0))
-    net.run(mixed + [sum_a, sum_b, sample(attention, 9)])
+    before = list(net.copies)
+
+    def settle():
+        yield net.now + 1.0
+        each(lambda j: token_copy(j).wait_send())
+        each(lambda j: query_copy(j).wait_send())
+        for made in before:
+            made.wait_send()
+
+    first_rows = [row_sum(team) for team in reversed(teams)]
+    net.run(first_rows[:1] + [sum_a()] + first_rows[1:] + [sum_b, sample(attention, 9), settle()])
 
     for i in range(n_seq):
         begin, turn = share * i // LANE * LANE, share * i % LANE
@@ -547,10 +555,8 @@
             total = total + erecv[2 * i + half].astype(F32)
         mix_out[half * HALF_TOK:(half + 1) * HALF_TOK, :] = total[:, 0:share].astype(BF16)
 
-    each(lambda j: token_copy(j).wait_send())
-    each(lambda j: query_copy(j).wait_send())
     each(lambda j: end_copy(j).wait_send())
-    for made in net.copies:
+    for made in net.copies[len(before):]:
         made.wait_send()
 
 
@@ -602,9 +608,9 @@
             pltpu.VMEM((rows, 2 * LANE), BF16),
             pltpu.VMEM((n_z, NX, HALF_TOK, wide_a), BF16),
             pltpu.VMEM((n_z, NX, HALF_TOK, wide_b), BF16),
-            pltpu.VMEM((NX, 2, far_z, HALF_TOK, wide_a), BF16),
+            pltpu.VMEM((2, far_z, NX, HALF_TOK, wide_a), BF16),
             pltpu.VMEM((2, far_x, HALF_TOK, wide_a), BF16),
-            pltpu.VMEM((n_z, 2, far_x, HALF_TOK, wide_b), BF16),
+            pltpu.VMEM((2, far_x, n_z, HALF_TOK, wide_b), BF16),
             pltpu.VMEM((2, far_z, HALF_TOK, wide_b), BF16),
             pltpu.VMEM((n_seq, HALF_TOK, padded), BF16),
             pltpu.VMEM((n_seq, HALF_TOK, padded), BF16),
@@ -617,8 +623,8 @@
             pltpu.VMEM((2, q_rows, LAT), BF16),
             pltpu.VMEM((q_rows, LAT), BF16),
             dma((5,)),
-            dma((200,)),
-            dma((200,)),
+            dma((120,)),
+            dma((120,)),
             dma((n_seq,)),
             dma((n_seq,)),
             dma((n_seq,)),

time: 104 us -> 103 us (level)
  Pallas kernels: 101 us -> 99 us
    pallas_call x1, Pallas kernels: 101 us -> 99 us  [on_device(): pl.pallas_call(functools.partial(kernel, cfg), out_shape=(jax.ShapeDtypeS...]
where the time goes in v3:
time: 103 us; the launch traced here: 102 us
  Pallas kernels  99 us (96%)
  local copies, waits for them, and re-layouts  2.8 us (3%)
    pallas_call x1, Pallas kernels, on_device(): pl.pallas_call(functools.partial(kernel, cfg), out_shape=(jax.ShapeDtypeS...  99 us
    unnamed x2, local copies, waits for them, and re-layouts  2.8 us

profile of v3, /device:TPU:1, one launch (start us, length us, event | category | flops | bytes accessed | tf_op | source)
XLA Modules:
  0.0 102.5 jit_solution(3923531336449988873)
XLA Ops:
  0.6 99.0 %shard_map.113 = (bf16[64,512]{1,0:T(8,128)(2,1)}, bf16[32,224]{1,0:T(8,128)(2,1)}) custom-call(bf16[8,576,128]{2,1,0:T(8,128)(2,1)} %bitcast.9, bf16[64,576]{1,0:T(8,128)(2,1)} %bitcast.13, bf16[3584,128]{1,0:T(8,128)(2,1)} %bitcast.10, bf16[3584,128]{1,0:T(8,128)(2,1)} %bitcast.11, bf16[128,3584]{1,0:T(8,128)(2,1)} %bitcast.12, s32[1,8]{1,0:T(1,128)} %lengths.1, ...), custom_call_target="tpu_custom_call" | custom-call | flops 2818572288 | bytes 6291456 | tf_op jit(solution)/shard_map/pallas_call | solution.py:590
  99.7 1.5 %copy.14 = bf16[8,8,512]{2,1,0:T(8,128)(2,1)} copy(bf16[8,8,512]{2,1,0:T(8,128)(2,1)} %bitcast.8) | data formatting | bytes 131072
  101.1 1.3 %copy.15 = bf16[32,224]{1,0:T(8,128)(2,1)} copy(bf16[32,224]{1,0:T(8,128)(2,1)} %get-tuple-element.9) | data formatting | bytes 28672

commit v4 on v3

--- a/solution.py
+++ b/solution.py
@@ -166,6 +166,7 @@
     other = 1 - c
     sibling = (2 * y + other, e)
     experts = n_z * NX
+    far_x = NX // 2
     n_req = lengths.shape[1]
     half_req = n_req // 2
     q_rows = half_req * heads
@@ -260,8 +261,6 @@
 
     net = Net(send_sem, recv_sem)
     each(lambda j: token_copy(j).start())
-    each(lambda j: query_copy(j).start())
-    lat_copy, _ = net.copy(latent.at[pl.ds(other * half_req, half_req)], lbuf.at[1], sibling, "core")
 
     tokbuf[s] = tokpad[c]
     line[...] = jnp.zeros_like(line)
@@ -340,7 +339,11 @@
         return carry
 
     def attend():
-        yield net.now + 8.0
+        lat_copy, _ = net.copy(
+            latent.at[pl.ds(other * half_req, half_req)], lbuf.at[1], sibling, "core"
+        )
+        each(lambda j: query_copy(j).start())
+        yield net.now + 12.0
         loads[0].wait()
         loads[1].wait()
         each(lambda j: query_copy(j).wait_recv())
@@ -381,6 +384,8 @@
 
     teams = [(0,)] + [(d, -d) for d in range(1, n_z // 2)] + [(n_z // 2,)]
 
+    pairs = [(i, i + 1) for i in range(0, NX, 2)]
+
     def slots(team):
         return pl.ds(slot_z[team[0]], len(team))
 
@@ -391,11 +396,22 @@
             landed[d] += 1
 
     def gather_a():
+        here = set()
+
+        def start(dx):
+            here.add(slot_x[dx])
+            for pair in pairs:
+                if slot_x[dx] in pair and here.issuperset(pair):
+                    net.add(net.now, along_z(pl.ds(pair[0], 2)))
+
+        def along_z(at):
+            return ring_gather(
+                net, lambda d: xa.at[slot_z[d], at], cut_a, n_z, z_up, z_down, "z",
+                lambda d: count((d,)),
+            )
+
         yield from ring_gather(
-            net, lambda d: xa.at[0, slot_x[d]], cut_a, NX, x_up, x_down, "x", lambda d: None
-        )
-        yield from ring_gather(
-            net, lambda d: xa.at[slot_z[d]], cut_a, n_z, z_up, z_down, "z", lambda d: count((d,))
+            net, lambda d: xa.at[0, slot_x[d]], cut_a, NX, x_up, x_down, "x", start
         )
 
     def gather_b():
@@ -414,7 +430,7 @@
             net, lambda d: xb.at[slot_z[d], 0], cut_b, n_z, z_up, z_down, "z", start
         )
 
-    step_a, step_b = wide_a // 3, wide_b // 4
+    step_a, step_b = wide_a // 2, wide_b // 3
     weights = []
 
     def load_weights():
@@ -437,7 +453,7 @@
 
         def up_b(k, carry):
             cols = pl.ds(pl.multiple_of(k * step_b, step_b), step_b)
-            down = pl.ds(pl.multiple_of(wide_a + k * step_b, step_b), step_b)
+            down = pl.ds(pl.multiple_of(wide_a + k * step_b, LANE), step_b)
             value = xb[first:last, :, :, cols].reshape(rows, step_b)
             acc[0:rows, :] += jnp.dot(value, wcat[down, :], preferred_element_type=F32)
             return carry
@@ -450,14 +466,14 @@
 
         def down_b(k, carry):
             cols = pl.ds(pl.multiple_of(k * step_b, step_b), step_b)
-            down = pl.ds(pl.multiple_of(wide_a + k * step_b, step_b), step_b)
+            down = pl.ds(pl.multiple_of(wide_a + k * step_b, LANE), step_b)
             value = jnp.dot(hid[0:rows, :], wdcat[:, down], preferred_element_type=F32)
             yb[first:last, :, :, cols] = value.astype(BF16).reshape(last - first, NX, HALF_TOK, step_b)
             return carry
 
         acc[0:rows, :] = jnp.zeros((rows, 4 * LANE), F32)
-        lax.fori_loop(0, 3, up_a, 0)
-        lax.fori_loop(0, 4, up_b, 0)
+        lax.fori_loop(0, 2, up_a, 0)
+        lax.fori_loop(0, 3, up_b, 0)
         tile = xb[first:last, :, :, wide_b:wide_b + LANE].reshape(rows, LANE).astype(F32)
         lane = lax.broadcasted_iota(jnp.int32, (rows, LANE), 1)
         gate = jnp.sum(
@@ -466,14 +482,14 @@
         g = acc[0:rows, 0:2 * LANE]
         value = g / (1.0 + jnp.exp(-g)) * acc[0:rows, 2 * LANE:4 * LANE] * gate
         hid[0:rows, :] = value.astype(BF16)
-        lax.fori_loop(0, 4, down_b, 0)
-        lax.fori_loop(0, 3, down_a, 0)
+        lax.fori_loop(0, 3, down_b, 0)
+        lax.fori_loop(0, 2, down_a, 0)
 
     def compute():
         offsets = around(n_z)
         groups = [(0, 3), (3, 5), (5, 7), (7, 8)] if n_z == 8 else [(0, len(offsets))]
         for first, last in groups:
-            while any(landed[d] < 1 + NX for d in offsets[first:last]):
+            while any(landed[d] < len(pairs) + NX for d in offsets[first:last]):
                 yield net.now + 0.01
             if first == 0:
                 for load in loads[2:]:
@@ -484,7 +500,7 @@
             net.now += 1.0
 
     attention = attend()
-    net.run([gather_a(), gather_b(), load_weights(), sample(attention, 3), compute()])
+    net.run([gather_a(), gather_b(), load_weights(), sample(attention, 4), compute()])
 
     net.links, net.now = {}, 0.0
     ended = set()
@@ -504,8 +520,19 @@
             NX, x_up, x_down, "x", always, finish,
         )
 
-    def keep_a(total):
-        ya[0] = total.astype(BF16)
+    done_a = set()
+
+    def column_sum(pair):
+        at = pl.ds(pair[0], 2)
+
+        def finish(total):
+            ya[0, at] = total.astype(BF16)
+            done_a.update(pair)
+
+        return ring_scatter(
+            net, lambda d: ya.at[slot_z[d], at], cut_a, lambda way, k: ra.at[way, k, at],
+            n_z, z_up, z_down, "z", always, finish,
+        )
 
     def end_a(total):
         line[:, 0:wide_a] = total
@@ -513,15 +540,10 @@
     def end_b(total):
         line[:, wide_a:wide_a + wide_b] = total
 
-    def sum_a():
-        yield from ring_scatter(
-            net, lambda d: ya.at[slot_z[d]], cut_a, lambda way, k: ra.at[way, k],
-            n_z, z_up, z_down, "z", always, keep_a,
-        )
-        yield from ring_scatter(
-            net, lambda d: ya.at[0, slot_x[d]], cut_a, lambda way, k: rax.at[way, k],
-            NX, x_up, x_down, "x", always, end_a,
-        )
+    sum_a = ring_scatter(
+        net, lambda d: ya.at[0, slot_x[d]], cut_a, lambda way, k: rax.at[way, k],
+        NX, x_up, x_down, "x", lambda d: slot_x[far_x if d == -far_x else d] in done_a, end_a,
+    )
 
     sum_b = ring_scatter(
         net, lambda d: yb.at[slot_z[d], 0], cut_b, lambda way, k: rb.at[way, k],
@@ -537,7 +559,8 @@
             made.wait_send()
 
     first_rows = [row_sum(team) for team in reversed(teams)]
-    net.run(first_rows[:1] + [sum_a()] + first_rows[1:] + [sum_b, sample(attention, 9), settle()])
+    columns = [column_sum(pair) for pair in reversed(pairs)]
+    net.run(first_rows[:1] + columns + first_rows[1:] + [sum_a, sum_b, sample(attention, 9), settle()])
 
     for i in range(n_seq):
         begin, turn = share * i // LANE * LANE, share * i % LANE
@@ -569,13 +592,22 @@
         yield ready
 
 
+def hand_out(context, mixed, context_out, mixed_out, sem):
+    first = pltpu.make_async_copy(context, context_out, sem.at[0])
+    second = pltpu.make_async_copy(mixed, mixed_out, sem.at[1])
+    first.start()
+    second.start()
+    first.wait()
+    second.wait()
+
+
 def on_device(latent, lengths, queries, fresh_latent, tokens, routes, gates, w_gate, w_up, w_down):
     n_seq, n_ep = lax.axis_size("seq"), lax.axis_size("ep")
     n_z, n_y = n_ep // NX, n_seq // 2
     n_req, heads, width = queries.shape
     share = tokens.shape[1]
     features = share * n_seq
-    wide_a = features // 7 * 3
+    wide_a = features // 14 * 5
     wide_b = features - wide_a
     padded = -(-share // LANE) * LANE
     rows = n_ep * HALF_TOK
@@ -648,6 +680,17 @@
         routes.T,
         gates.T,
     )
+    context, mixed = pl.pallas_call(
+        hand_out,
+        out_shape=(
+            jax.ShapeDtypeStruct(context.shape, BF16),
+            jax.ShapeDtypeStruct(mixed.shape, BF16),
+        ),
+        in_specs=[hbm, hbm],
+        out_specs=(hbm, hbm),
+        scratch_shapes=[dma((2,))],
+        compiler_params=pltpu.CompilerParams(vmem_limit_bytes=60 * 1024 * 1024),
+    )(context, mixed)
     return context.reshape(n_req, heads, LAT), mixed
 
 

time: 103 us -> 106 us (1.029)
  Pallas kernels: 99 us -> 105 us
  local copies, waits for them, and re-layouts: 2.8 us -> 0 us
    pallas_call x0 -> x1, Pallas kernels: none -> 3.6 us  [on_device(): pl.pallas_call(hand_out, out_shape=(jax.ShapeDtypeStruct(context.shape, B...]
    unnamed x2 -> x0, local copies, waits for them, and re-layouts: 2.8 us -> none
    pallas_call x1, Pallas kernels: 99 us -> 101 us  [on_device(): pl.pallas_call(functools.partial(kernel, cfg), out_shape=(jax.ShapeDtypeS...]
where the time goes in v4:
time: 106 us
  Pallas kernels  105 us (99%)
    pallas_call x1, Pallas kernels, on_device(): pl.pallas_call(functools.partial(kernel, cfg), out_shape=(jax.ShapeDtypeS...  101 us
    pallas_call x1, Pallas kernels, on_device(): pl.pallas_call(hand_out, out_shape=(jax.ShapeDtypeStruct(context.shape, B...  3.6 us

profile of v4, /device:TPU:1, one launch (start us, length us, event | category | flops | bytes accessed | tf_op | source)
XLA Modules:
  0.0 105.6 jit_solution(13832468028358223803)
XLA Ops:
  0.6 101.4 %shard_map.113 = (bf16[64,512]{1,0:T(8,128)(2,1)}, bf16[32,224]{1,0:T(8,128)(2,1)}) custom-call(bf16[8,576,128]{2,1,0:T(8,128)(2,1)} %bitcast.8, bf16[64,576]{1,0:T(8,128)(2,1)} %bitcast.12, bf16[3584,128]{1,0:T(8,128)(2,1)} %bitcast.9, bf16[3584,128]{1,0:T(8,128)(2,1)} %bitcast.10, bf16[128,3584]{1,0:T(8,128)(2,1)} %bitcast.11, s32[1,8]{1,0:T(1,128)} %lengths.1, ...), custom_call_target="tpu_custom_call" | custom-call | flops 2818572288 | bytes 6291456 | tf_op jit(solution)/shard_map/pallas_call | solution.py:622
  102.0 3.6 %shard_map.114 = (bf16[64,512]{1,0:T(8,128)(2,1)}, bf16[32,224]{1,0:T(8,128)(2,1)}) custom-call(bf16[64,512]{1,0:T(8,128)(2,1)} %get-tuple-element.6.context, bf16[32,224]{1,0:T(8,128)(2,1)} %get-tuple-element.7.mixed), custom_call_target="tpu_custom_call" | custom-call | tf_op jit(solution)/shard_map/pallas_call | solution.py:683

commit v5 on v4

--- a/solution.py
+++ b/solution.py
@@ -430,7 +430,7 @@
             net, lambda d: xb.at[slot_z[d], 0], cut_b, n_z, z_up, z_down, "z", start
         )
 
-    step_a, step_b = wide_a // 2, wide_b // 3
+    step_a, step_b = wide_a // 3, wide_b // 2
     weights = []
 
     def load_weights():
@@ -472,8 +472,8 @@
             return carry
 
         acc[0:rows, :] = jnp.zeros((rows, 4 * LANE), F32)
-        lax.fori_loop(0, 2, up_a, 0)
-        lax.fori_loop(0, 3, up_b, 0)
+        lax.fori_loop(0, 3, up_a, 0)
+        lax.fori_loop(0, 2, up_b, 0)
         tile = xb[first:last, :, :, wide_b:wide_b + LANE].reshape(rows, LANE).astype(F32)
         lane = lax.broadcasted_iota(jnp.int32, (rows, LANE), 1)
         gate = jnp.sum(
@@ -482,8 +482,8 @@
         g = acc[0:rows, 0:2 * LANE]
         value = g / (1.0 + jnp.exp(-g)) * acc[0:rows, 2 * LANE:4 * LANE] * gate
         hid[0:rows, :] = value.astype(BF16)
-        lax.fori_loop(0, 3, down_b, 0)
-        lax.fori_loop(0, 2, down_a, 0)
+        lax.fori_loop(0, 2, down_b, 0)
+        lax.fori_loop(0, 3, down_a, 0)
 
     def compute():
         offsets = around(n_z)
@@ -592,22 +592,13 @@
         yield ready
 
 
-def hand_out(context, mixed, context_out, mixed_out, sem):
-    first = pltpu.make_async_copy(context, context_out, sem.at[0])
-    second = pltpu.make_async_copy(mixed, mixed_out, sem.at[1])
-    first.start()
-    second.start()
-    first.wait()
-    second.wait()
-
-
 def on_device(latent, lengths, queries, fresh_latent, tokens, routes, gates, w_gate, w_up, w_down):
     n_seq, n_ep = lax.axis_size("seq"), lax.axis_size("ep")
     n_z, n_y = n_ep // NX, n_seq // 2
     n_req, heads, width = queries.shape
     share = tokens.shape[1]
     features = share * n_seq
-    wide_a = features // 14 * 5
+    wide_a = features // 14 * 9
     wide_b = features - wide_a
     padded = -(-share // LANE) * LANE
     rows = n_ep * HALF_TOK
@@ -680,17 +671,6 @@
         routes.T,
         gates.T,
     )
-    context, mixed = pl.pallas_call(
-        hand_out,
-        out_shape=(
-            jax.ShapeDtypeStruct(context.shape, BF16),
-            jax.ShapeDtypeStruct(mixed.shape, BF16),
-        ),
-        in_specs=[hbm, hbm],
-        out_specs=(hbm, hbm),
-        scratch_shapes=[dma((2,))],
-        compiler_params=pltpu.CompilerParams(vmem_limit_bytes=60 * 1024 * 1024),
-    )(context, mixed)
     return context.reshape(n_req, heads, LAT), mixed
 
 

time: 106 us -> 109 us (1.028)
  local copies, waits for them, and re-layouts: 0 us -> 2.8 us
    pallas_call x1 -> x0, Pallas kernels: 3.6 us -> none  [on_device(): pl.pallas_call(hand_out, out_shape=(jax.ShapeDtypeStruct(context.shape, B...]
    pallas_call x1, Pallas kernels: 101 us -> 105 us  [on_device(): pl.pallas_call(functools.partial(kernel, cfg), out_shape=(jax.ShapeDtypeS...]
    unnamed x0 -> x2, local copies, waits for them, and re-layouts: none -> 2.8 us
where the time goes in v5:
time: 109 us; the launch traced here: 108 us
  Pallas kernels  105 us (96%)
  local copies, waits for them, and re-layouts  2.8 us (3%)
    pallas_call x1, Pallas kernels, on_device(): pl.pallas_call(functools.partial(kernel, cfg), out_shape=(jax.ShapeDtypeS...  105 us
    unnamed x2, local copies, waits for them, and re-layouts  2.8 us

profile of v5, /device:TPU:1, one launch (start us, length us, event | category | flops | bytes accessed | tf_op | source)
XLA Modules:
  0.0 108.4 jit_solution(14409641812512131513)
XLA Ops:
  0.6 105.0 %shard_map.113 = (bf16[64,512]{1,0:T(8,128)(2,1)}, bf16[32,224]{1,0:T(8,128)(2,1)}) custom-call(bf16[8,576,128]{2,1,0:T(8,128)(2,1)} %bitcast.9, bf16[64,576]{1,0:T(8,128)(2,1)} %bitcast.13, bf16[3584,128]{1,0:T(8,128)(2,1)} %bitcast.10, bf16[3584,128]{1,0:T(8,128)(2,1)} %bitcast.11, bf16[128,3584]{1,0:T(8,128)(2,1)} %bitcast.12, s32[1,8]{1,0:T(1,128)} %lengths.1, ...), custom_call_target="tpu_custom_call" | custom-call | flops 2818572288 | bytes 6291456 | tf_op jit(solution)/shard_map/pallas_call | solution.py:613
  105.6 1.5 %copy.14 = bf16[8,8,512]{2,1,0:T(8,128)(2,1)} copy(bf16[8,8,512]{2,1,0:T(8,128)(2,1)} %bitcast.8) | data formatting | bytes 131072
  107.1 1.3 %copy.15 = bf16[32,224]{1,0:T(8,128)(2,1)} copy(bf16[32,224]{1,0:T(8,128)(2,1)} %get-tuple-element.9) | data formatting | bytes 28672

commit v6 on v5

--- a/solution.py
+++ b/solution.py
@@ -261,6 +261,16 @@
 
     net = Net(send_sem, recv_sem)
     each(lambda j: token_copy(j).start())
+    lat_copy, _ = net.copy(latent.at[pl.ds(other * half_req, half_req)], lbuf.at[1], sibling, "core")
+    weights = [
+        net.copy(src, dst, sibling, "core")[0]
+        for src, dst in (
+            (wg, wcat.at[:, pl.ds(LANE, LANE)]),
+            (wu, wcat.at[:, pl.ds(3 * LANE, LANE)]),
+            (wd, wdcat.at[pl.ds(LANE, LANE)]),
+        )
+    ]
+    each(lambda j: query_copy(j).start())
 
     tokbuf[s] = tokpad[c]
     line[...] = jnp.zeros_like(line)
@@ -339,11 +349,7 @@
         return carry
 
     def attend():
-        lat_copy, _ = net.copy(
-            latent.at[pl.ds(other * half_req, half_req)], lbuf.at[1], sibling, "core"
-        )
-        each(lambda j: query_copy(j).start())
-        yield net.now + 12.0
+        yield net.now + 8.0
         loads[0].wait()
         loads[1].wait()
         each(lambda j: query_copy(j).wait_recv())
@@ -430,18 +436,7 @@
             net, lambda d: xb.at[slot_z[d], 0], cut_b, n_z, z_up, z_down, "z", start
         )
 
-    step_a, step_b = wide_a // 3, wide_b // 2
-    weights = []
-
-    def load_weights():
-        yield net.now + 0.5
-        for src, dst in (
-            (wg, wcat.at[:, pl.ds(LANE, LANE)]),
-            (wu, wcat.at[:, pl.ds(3 * LANE, LANE)]),
-            (wd, wdcat.at[pl.ds(LANE, LANE)]),
-        ):
-            weights.append(net.copy(src, dst, sibling, "core")[0])
-
+    step_a, step_b = wide_a // 3, wide_b // 4
     def experts_of(first, last):
         rows = (last - first) * NX * HALF_TOK
 
@@ -473,7 +468,7 @@
 
         acc[0:rows, :] = jnp.zeros((rows, 4 * LANE), F32)
         lax.fori_loop(0, 3, up_a, 0)
-        lax.fori_loop(0, 2, up_b, 0)
+        lax.fori_loop(0, 4, up_b, 0)
         tile = xb[first:last, :, :, wide_b:wide_b + LANE].reshape(rows, LANE).astype(F32)
         lane = lax.broadcasted_iota(jnp.int32, (rows, LANE), 1)
         gate = jnp.sum(
@@ -482,7 +477,7 @@
         g = acc[0:rows, 0:2 * LANE]
         value = g / (1.0 + jnp.exp(-g)) * acc[0:rows, 2 * LANE:4 * LANE] * gate
         hid[0:rows, :] = value.astype(BF16)
-        lax.fori_loop(0, 2, down_b, 0)
+        lax.fori_loop(0, 4, down_b, 0)
         lax.fori_loop(0, 3, down_a, 0)
 
     def compute():
@@ -500,7 +495,7 @@
             net.now += 1.0
 
     attention = attend()
-    net.run([gather_a(), gather_b(), load_weights(), sample(attention, 4), compute()])
+    net.run([gather_a(), gather_b(), sample(attention, 3), compute()])
 
     net.links, net.now = {}, 0.0
     ended = set()
@@ -598,7 +593,7 @@
     n_req, heads, width = queries.shape
     share = tokens.shape[1]
     features = share * n_seq
-    wide_a = features // 14 * 9
+    wide_a = features // 7 * 3
     wide_b = features - wide_a
     padded = -(-share // LANE) * LANE
     rows = n_ep * HALF_TOK

time: 109 us -> 104 us (0.954)
  Pallas kernels: 105 us -> 100 us
    pallas_call x1, Pallas kernels: 105 us -> 100 us  [on_device(): pl.pallas_call(functools.partial(kernel, cfg), out_shape=(jax.ShapeDtypeS...]
where the time goes in v6:
time: 104 us
  Pallas kernels  100 us (96%)
  local copies, waits for them, and re-layouts  2.8 us (3%)
    pallas_call x1, Pallas kernels, on_device(): pl.pallas_call(functools.partial(kernel, cfg), out_shape=(jax.ShapeDtypeS...  100 us
    unnamed x2, local copies, waits for them, and re-layouts  2.8 us

profile of v6, /device:TPU:1, one launch (start us, length us, event | category | flops | bytes accessed | tf_op | source)
XLA Modules:
  0.0 103.5 jit_solution(567439673352259523)
XLA Ops:
  0.6 100.1 %shard_map.113 = (bf16[64,512]{1,0:T(8,128)(2,1)}, bf16[32,224]{1,0:T(8,128)(2,1)}) custom-call(bf16[8,576,128]{2,1,0:T(8,128)(2,1)} %bitcast.9, bf16[64,576]{1,0:T(8,128)(2,1)} %bitcast.13, bf16[3584,128]{1,0:T(8,128)(2,1)} %bitcast.10, bf16[3584,128]{1,0:T(8,128)(2,1)} %bitcast.11, bf16[128,3584]{1,0:T(8,128)(2,1)} %bitcast.12, s32[1,8]{1,0:T(1,128)} %lengths.1, ...), custom_call_target="tpu_custom_call" | custom-call | flops 2818572288 | bytes 6291456 | tf_op jit(solution)/shard_map/pallas_call | solution.py:608
  100.7 1.5 %copy.14 = bf16[8,8,512]{2,1,0:T(8,128)(2,1)} copy(bf16[8,8,512]{2,1,0:T(8,128)(2,1)} %bitcast.8) | data formatting | bytes 131072
  102.2 1.3 %copy.15 = bf16[32,224]{1,0:T(8,128)(2,1)} copy(bf16[32,224]{1,0:T(8,128)(2,1)} %get-tuple-element.9) | data formatting | bytes 28672

commit v7 on v6

--- a/solution.py
+++ b/solution.py
@@ -32,7 +32,7 @@
         self.count, self.now = 0, 0.0
         self.links, self.copies = {}, []
 
-    def copy(self, src, dst, device, link):
+    def copy(self, src, dst, device, link, hops=1):
         at = self.count
         self.count += 1
         made = pltpu.make_async_remote_copy(
@@ -44,7 +44,7 @@
             device_id_type=MESH,
         )
         made.start()
-        size = 2
+        size = 2 * hops
         for extent in src.shape:
             size *= extent
         begin = max(self.links.get(link, 0.0), self.now)
@@ -102,6 +102,82 @@
     cu.wait_recv()
     cd.wait_recv()
     landed(far)
+
+
+def skip_gather(net, piece, cut, ups, downs, axis, landed):
+    def send(src, at, way, hops, side=None):
+        dst = piece(at)
+        if side is not None:
+            src, dst = cut(src, side), cut(dst, side)
+        return net.copy(src, dst, way[hops - 1], axis + ("+" if way is ups else "-"), hops)
+
+    c2u, t2u = send(piece(0), -2, ups, 2)
+    c2d, t2d = send(piece(0), 2, downs, 2)
+    c1u, t1u = send(piece(0), -1, ups, 1)
+    c1d, t1d = send(piece(0), 1, downs, 1)
+    landed(0)
+    yield t2u
+    c2u.wait_recv()
+    c4u, t4u = send(piece(-2), 4, ups, 2, 0)
+    c3u, t3u = send(piece(-2), -3, ups, 1)
+    landed(-2)
+    yield t2d
+    c2d.wait_recv()
+    c4d, t4d = send(piece(2), 4, downs, 2, 1)
+    c3d, t3d = send(piece(2), 3, downs, 1)
+    landed(2)
+    yield t1u
+    c1u.wait_recv()
+    landed(-1)
+    yield t1d
+    c1d.wait_recv()
+    landed(1)
+    yield max(t3u, t3d)
+    c3u.wait_recv()
+    landed(-3)
+    c3d.wait_recv()
+    landed(3)
+    yield max(t4u, t4d)
+    c4u.wait_recv()
+    c4d.wait_recv()
+    landed(4)
+
+
+def skip_scatter(net, piece, cut, arrived, ups, downs, axis, ready, finish):
+    up, down = axis + "+", axis + "-"
+    while not (ready(4) and ready(3) and ready(-3)):
+        yield net.now + 0.01
+    c4u, t4u = net.copy(cut(piece(4), 0), cut(arrived(0, 0), 0), ups[1], up, 2)
+    c4d, t4d = net.copy(cut(piece(4), 1), cut(arrived(1, 0), 1), downs[1], down, 2)
+    c3u, t3u = net.copy(piece(3), arrived(0, 1), ups[0], up)
+    c3d, t3d = net.copy(piece(-3), arrived(1, 1), downs[0], down)
+    while not (ready(2) and ready(-2)):
+        yield net.now + 0.01
+    yield max(t4u, t3u)
+    c4u.wait_recv()
+    c3u.wait_recv()
+    add_into(cut(piece(2), 0), cut(arrived(0, 0), 0))
+    add_into(piece(2), arrived(0, 1))
+    c2u, t2u = net.copy(piece(2), arrived(0, 2), ups[1], up, 2)
+    yield max(t4d, t3d)
+    c4d.wait_recv()
+    c3d.wait_recv()
+    add_into(cut(piece(-2), 1), cut(arrived(1, 0), 1))
+    add_into(piece(-2), arrived(1, 1))
+    c2d, t2d = net.copy(piece(-2), arrived(1, 2), downs[1], down, 2)
+    while not (ready(1) and ready(-1)):
+        yield net.now + 0.01
+    c1u, t1u = net.copy(piece(1), arrived(0, 3), ups[0], up)
+    c1d, t1d = net.copy(piece(-1), arrived(1, 3), downs[0], down)
+    while not ready(0):
+        yield net.now + 0.01
+    yield max(t2u, t2d, t1u, t1d)
+    total = piece(0)[...].astype(F32)
+    for k, (one, two) in ((3, (c1u, c1d)), (2, (c2u, c2d))):
+        one.wait_recv()
+        two.wait_recv()
+        total = total + arrived(0, k)[...].astype(F32) + arrived(1, k)[...].astype(F32)
+    finish(total)
 
 
 def add_into(ref, other):
@@ -172,6 +248,8 @@
     q_rows = half_req * heads
     x_up, x_down = (s, z * NX + mod(x + 1, NX)), (s, z * NX + mod(x - 1, NX))
     z_up, z_down = (s, mod(z + 1, n_z) * NX + x), (s, mod(z - 1, n_z) * NX + x)
+    z_ups = (z_up, (s, mod(z + 2, n_z) * NX + x))
+    z_downs = (z_down, (s, mod(z - 2, n_z) * NX + x))
     slot_z = {d: i for i, d in enumerate(around(n_z))}
     slot_x = {d: i for i, d in enumerate(around(NX))}
 
@@ -193,7 +271,7 @@
         return carry
 
     lax.fori_loop(1, n_seq, greet, 0)
-    for who in (x_up, x_down, z_up, z_down):
+    for who in (x_up, x_down) + z_ups + z_downs:
         pl.semaphore_signal(barrier, inc=1, device_id=who, device_id_type=MESH)
 
     mine_q = queries.at[pl.ds(pl.multiple_of(c * q_rows, q_rows), q_rows)]
@@ -216,7 +294,7 @@
     square[:, 0:routes.shape[1]] = weight
     square[...] = jnp.transpose(square[...])
 
-    pl.semaphore_wait(barrier, n_seq - 1 + 4)
+    pl.semaphore_wait(barrier, n_seq - 1 + 6)
 
     def token_copy(j):
         to = lax.rem(s + j, n_seq)
@@ -395,6 +473,16 @@
     def slots(team):
         return pl.ds(slot_z[team[0]], len(team))
 
+    def gather_z(piece, cut, done):
+        if n_z == 8:
+            return skip_gather(net, piece, cut, z_ups, z_downs, "z", done)
+        return ring_gather(net, piece, cut, n_z, z_up, z_down, "z", done)
+
+    def scatter_z(piece, cut, arrived, ready, finish):
+        if n_z == 8:
+            return skip_scatter(net, piece, cut, arrived, z_ups, z_downs, "z", ready, finish)
+        return ring_scatter(net, piece, cut, arrived, n_z, z_up, z_down, "z", ready, finish)
+
     landed = {d: 0 for d in slot_z}
 
     def count(team):
@@ -411,10 +499,7 @@
                     net.add(net.now, along_z(pl.ds(pair[0], 2)))
 
         def along_z(at):
-            return ring_gather(
-                net, lambda d: xa.at[slot_z[d], at], cut_a, n_z, z_up, z_down, "z",
-                lambda d: count((d,)),
-            )
+            return gather_z(lambda d: xa.at[slot_z[d], at], cut_a, lambda d: count((d,)))
 
         yield from ring_gather(
             net, lambda d: xa.at[0, slot_x[d]], cut_a, NX, x_up, x_down, "x", start
@@ -432,11 +517,9 @@
                     lambda d: count(team),
                 ))
 
-        yield from ring_gather(
-            net, lambda d: xb.at[slot_z[d], 0], cut_b, n_z, z_up, z_down, "z", start
-        )
-
-    step_a, step_b = wide_a // 3, wide_b // 4
+        yield from gather_z(lambda d: xb.at[slot_z[d], 0], cut_b, start)
+
+    step_a, step_b = wide_a // 2, wide_b // 5
     def experts_of(first, last):
         rows = (last - first) * NX * HALF_TOK
 
@@ -467,8 +550,8 @@
             return carry
 
         acc[0:rows, :] = jnp.zeros((rows, 4 * LANE), F32)
-        lax.fori_loop(0, 3, up_a, 0)
-        lax.fori_loop(0, 4, up_b, 0)
+        lax.fori_loop(0, 2, up_a, 0)
+        lax.fori_loop(0, 5, up_b, 0)
         tile = xb[first:last, :, :, wide_b:wide_b + LANE].reshape(rows, LANE).astype(F32)
         lane = lax.broadcasted_iota(jnp.int32, (rows, LANE), 1)
         gate = jnp.sum(
@@ -477,12 +560,12 @@
         g = acc[0:rows, 0:2 * LANE]
         value = g / (1.0 + jnp.exp(-g)) * acc[0:rows, 2 * LANE:4 * LANE] * gate
         hid[0:rows, :] = value.astype(BF16)
-        lax.fori_loop(0, 4, down_b, 0)
-        lax.fori_loop(0, 3, down_a, 0)
+        lax.fori_loop(0, 5, down_b, 0)
+        lax.fori_loop(0, 2, down_a, 0)
 
     def compute():
         offsets = around(n_z)
-        groups = [(0, 3), (3, 5), (5, 7), (7, 8)] if n_z == 8 else [(0, len(offsets))]
+        groups = [(0, 5), (5, 8)] if n_z == 8 else [(0, len(offsets))]
         for first, last in groups:
             while any(landed[d] < len(pairs) + NX for d in offsets[first:last]):
                 yield net.now + 0.01
@@ -524,9 +607,8 @@
             ya[0, at] = total.astype(BF16)
             done_a.update(pair)
 
-        return ring_scatter(
-            net, lambda d: ya.at[slot_z[d], at], cut_a, lambda way, k: ra.at[way, k, at],
-            n_z, z_up, z_down, "z", always, finish,
+        return scatter_z(
+            lambda d: ya.at[slot_z[d], at], cut_a, lambda way, k: ra.at[way, k, at], always, finish
         )
 
     def end_a(total):
@@ -540,9 +622,9 @@
         NX, x_up, x_down, "x", lambda d: slot_x[far_x if d == -far_x else d] in done_a, end_a,
     )
 
-    sum_b = ring_scatter(
-        net, lambda d: yb.at[slot_z[d], 0], cut_b, lambda way, k: rb.at[way, k],
-        n_z, z_up, z_down, "z", lambda d: d in ended, end_b,
+    sum_b = scatter_z(
+        lambda d: yb.at[slot_z[d], 0], cut_b, lambda way, k: rb.at[way, k],
+        lambda d: d in ended, end_b,
     )
     before = list(net.copies)
 
@@ -593,7 +675,7 @@
     n_req, heads, width = queries.shape
     share = tokens.shape[1]
     features = share * n_seq
-    wide_a = features // 7 * 3
+    wide_a = features // 7 * 2
     wide_b = features - wide_a
     padded = -(-share // LANE) * LANE
     rows = n_ep * HALF_TOK

time: 104 us -> 104 us (level)
  no operation moved by 1% of the time
where the time goes in v7:
time: 104 us
  Pallas kernels  101 us (97%)
  local copies, waits for them, and re-layouts  2.8 us (3%)
    pallas_call x1, Pallas kernels, on_device(): pl.pallas_call(functools.partial(kernel, cfg), out_shape=(jax.ShapeDtypeS...  101 us
    unnamed x2, local copies, waits for them, and re-layouts  2.8 us

profile of v7, /device:TPU:1, one launch (start us, length us, event | category | flops | bytes accessed | tf_op | source)
XLA Modules:
  0.0 104.2 jit_solution(15143582971318173603)
XLA Ops:
  0.6 100.8 %shard_map.113 = (bf16[64,512]{1,0:T(8,128)(2,1)}, bf16[32,224]{1,0:T(8,128)(2,1)}) custom-call(bf16[8,576,128]{2,1,0:T(8,128)(2,1)} %bitcast.9, bf16[64,576]{1,0:T(8,128)(2,1)} %bitcast.13, bf16[3584,128]{1,0:T(8,128)(2,1)} %bitcast.10, bf16[3584,128]{1,0:T(8,128)(2,1)} %bitcast.11, bf16[128,3584]{1,0:T(8,128)(2,1)} %bitcast.12, s32[1,8]{1,0:T(1,128)} %lengths.1, ...), custom_call_target="tpu_custom_call" | custom-call | flops 2818572288 | bytes 6291456 | tf_op jit(solution)/shard_map/pallas_call | solution.py:690
  101.4 1.5 %copy.14 = bf16[8,8,512]{2,1,0:T(8,128)(2,1)} copy(bf16[8,8,512]{2,1,0:T(8,128)(2,1)} %bitcast.8) | data formatting | bytes 131072
  102.9 1.3 %copy.15 = bf16[32,224]{1,0:T(8,128)(2,1)} copy(bf16[32,224]{1,0:T(8,128)(2,1)} %get-tuple-element.9) | data formatting | bytes 28672

commit v8 on v7

--- a/solution.py
+++ b/solution.py
@@ -231,7 +231,7 @@
     ctx_out, mix_out,
     tokpad, tokbuf, line, square, xa, xb, wcat, wdcat, acc, hid, ya, yb,
     ra, rax, rbx, rb, ebuf, erecv,
-    lbuf, qbuf, qf, obuf, orecv, cf, cb, crecv,
+    lbuf, qpad, qbuf, qf, obuf, orecv, cf, cb, crecv,
     local_sem, send_sem, recv_sem, t_send, t_recv, q_send, q_recv, e_send, e_recv,
 ):
     n_seq, n_z, wide_a, wide_b, share, heads = cfg
@@ -262,6 +262,11 @@
         tokpad[half] = jnp.zeros_like(tokpad[half])
         tokpad[half, :, 0:share] = tokens[half * HALF_TOK:(half + 1) * HALF_TOK, :]
 
+    width = queries.shape[1]
+    for half in range(2):
+        qpad[half] = jnp.zeros_like(qpad[half])
+        qpad[half, :, 0:width] = queries[half * q_rows:(half + 1) * q_rows, :]
+
     barrier = pltpu.get_barrier_semaphore()
 
     def greet(j, carry):
@@ -274,13 +279,11 @@
     for who in (x_up, x_down) + z_ups + z_downs:
         pl.semaphore_signal(barrier, inc=1, device_id=who, device_id_type=MESH)
 
-    mine_q = queries.at[pl.ds(pl.multiple_of(c * q_rows, q_rows), q_rows)]
     loads = [
-        local(mine_q, qbuf.at[s], 0),
-        local(latent.at[pl.ds(c * half_req, half_req)], lbuf.at[0], 1),
-        local(wg, wcat.at[:, pl.ds(0, LANE)], 2),
-        local(wu, wcat.at[:, pl.ds(2 * LANE, LANE)], 3),
-        local(wd, wdcat.at[pl.ds(0, LANE)], 4),
+        local(latent.at[pl.ds(c * half_req, half_req)], lbuf.at[0], 0),
+        local(wg, wcat.at[0], 1),
+        local(wu, wcat.at[2], 2),
+        local(wd, wdcat.at[pl.ds(0, LANE)], 3),
     ]
 
     row = lax.broadcasted_iota(jnp.int32, (LANE, routes.shape[1]), 0)
@@ -309,9 +312,8 @@
 
     def query_copy(j):
         to = lax.rem(s + j, n_seq)
-        begin = pl.multiple_of(lax.rem(to, 2) * q_rows, q_rows)
         return pltpu.make_async_remote_copy(
-            src_ref=queries.at[pl.ds(begin, q_rows)],
+            src_ref=qpad.at[lax.rem(to, 2)],
             dst_ref=qbuf.at[s],
             send_sem=q_send.at[j],
             recv_sem=q_recv.at[j],
@@ -343,14 +345,15 @@
     weights = [
         net.copy(src, dst, sibling, "core")[0]
         for src, dst in (
-            (wg, wcat.at[:, pl.ds(LANE, LANE)]),
-            (wu, wcat.at[:, pl.ds(3 * LANE, LANE)]),
+            (wg, wcat.at[1]),
+            (wu, wcat.at[3]),
             (wd, wdcat.at[pl.ds(LANE, LANE)]),
         )
     ]
     each(lambda j: query_copy(j).start())
 
     tokbuf[s] = tokpad[c]
+    qbuf[s] = qpad[c]
     line[...] = jnp.zeros_like(line)
     first_row = pl.multiple_of(c * HALF_TOK, HALF_TOK)
     xb[0, 0, :, wide_b:wide_b + LANE] = square[pl.ds(first_row, HALF_TOK), :].astype(BF16)
@@ -429,10 +432,9 @@
     def attend():
         yield net.now + 8.0
         loads[0].wait()
-        loads[1].wait()
         each(lambda j: query_copy(j).wait_recv())
         lat_copy.wait_recv()
-        qf[...] = qbuf[...].astype(F32)
+        qf[...] = qbuf[:, :, 0:width].astype(F32)
         lax.fori_loop(0, half_req // 2, one_request, 0)
         net.now += 2.0
         yield net.now + 0.5
@@ -523,17 +525,20 @@
     def experts_of(first, last):
         rows = (last - first) * NX * HALF_TOK
 
+        def beside(some):
+            return jnp.concatenate([wcat[i, some, :] for i in range(4)], axis=1)
+
         def up_a(k, carry):
             cols = pl.ds(pl.multiple_of(k * step_a, step_a), step_a)
             value = xa[first:last, :, :, cols].reshape(rows, step_a)
-            acc[0:rows, :] += jnp.dot(value, wcat[cols, :], preferred_element_type=F32)
+            acc[0:rows, :] += jnp.dot(value, beside(cols), preferred_element_type=F32)
             return carry
 
         def up_b(k, carry):
             cols = pl.ds(pl.multiple_of(k * step_b, step_b), step_b)
             down = pl.ds(pl.multiple_of(wide_a + k * step_b, LANE), step_b)
             value = xb[first:last, :, :, cols].reshape(rows, step_b)
-            acc[0:rows, :] += jnp.dot(value, wcat[down, :], preferred_element_type=F32)
+            acc[0:rows, :] += jnp.dot(value, beside(down), preferred_element_type=F32)
             return carry
 
         def down_a(k, carry):
@@ -570,7 +575,7 @@
             while any(landed[d] < len(pairs) + NX for d in offsets[first:last]):
                 yield net.now + 0.01
             if first == 0:
-                for load in loads[2:]:
+                for load in loads[1:]:
                     load.wait()
                 for made in weights:
                     made.wait_recv()
@@ -678,6 +683,7 @@
     wide_a = features // 7 * 2
     wide_b = features - wide_a
     padded = -(-share // LANE) * LANE
+    wide_q = -(-width // LANE) * LANE
     rows = n_ep * HALF_TOK
     half_req = n_req // 2
     q_rows = half_req * heads
@@ -693,7 +699,7 @@
             jax.ShapeDtypeStruct((n_req * heads, LAT), BF16),
             jax.ShapeDtypeStruct(tokens.shape, BF16),
         ),
-        in_specs=[hbm, hbm, hbm, hbm, hbm, pl.BlockSpec(memory_space=pltpu.SMEM), vmem, vmem, vmem, vmem],
+        in_specs=[hbm, vmem, hbm, hbm, hbm, pl.BlockSpec(memory_space=pltpu.SMEM), vmem, vmem, vmem, vmem],
         out_specs=(vmem, vmem),
         scratch_shapes=[
             pltpu.VMEM((2, HALF_TOK, padded), BF16),
@@ -702,7 +708,7 @@
             pltpu.VMEM((LANE, LANE), F32),
             pltpu.VMEM((n_z, NX, HALF_TOK, wide_a), BF16),
             pltpu.VMEM((n_z, NX, HALF_TOK, wide_b + LANE), BF16),
-            pltpu.VMEM((features, 4 * LANE), BF16),
+            pltpu.VMEM((4, features, LANE), BF16),
             pltpu.VMEM((2 * LANE, features), BF16),
             pltpu.VMEM((rows, 4 * LANE), F32),
             pltpu.VMEM((rows, 2 * LANE), BF16),
@@ -715,14 +721,15 @@
             pltpu.VMEM((n_seq, HALF_TOK, padded), BF16),
             pltpu.VMEM((n_seq, HALF_TOK, padded), BF16),
             pltpu.VMEM((2, half_req, width, LANE), BF16),
-            pltpu.VMEM((n_seq, q_rows, width), BF16),
+            pltpu.VMEM((2, q_rows, wide_q), BF16),
+            pltpu.VMEM((n_seq, q_rows, wide_q), BF16),
             pltpu.VMEM((n_seq, q_rows, width), F32),
             pltpu.VMEM((n_y, 2 * q_rows, LAT + LANE), BF16),
             pltpu.VMEM((n_y, 2 * q_rows, LAT + LANE), BF16),
             pltpu.VMEM((2, q_rows, LAT), F32),
             pltpu.VMEM((2, q_rows, LAT), BF16),
             pltpu.VMEM((q_rows, LAT), BF16),
-            dma((5,)),
+            dma((4,)),
             dma((120,)),
             dma((120,)),
             dma((n_seq,)),

time: 104 us -> 105 us (level)
  no operation moved by 1% of the time
where the time goes in v8:
time: 105 us; the launch traced here: 104 us
  Pallas kernels  101 us (96%)
  local copies, waits for them, and re-layouts  2.8 us (3%)
    pallas_call x1, Pallas kernels, on_device(): pl.pallas_call(functools.partial(kernel, cfg), out_shape=(jax.ShapeDtypeS...  101 us
    unnamed x2, local copies, waits for them, and re-layouts  2.8 us

profile of v8, /device:TPU:1, one launch (start us, length us, event | category | flops | bytes accessed | tf_op | source)
XLA Modules:
  0.0 104.3 jit_solution(10645248126496000651)
XLA Ops:
  0.6 100.9 %shard_map.113 = (bf16[64,512]{1,0:T(8,128)(2,1)}, bf16[32,224]{1,0:T(8,128)(2,1)}) custom-call(bf16[8,576,128]{2,1,0:T(8,128)(2,1)} %bitcast.9, bf16[64,576]{1,0:T(8,128)(2,1)} %bitcast.13, bf16[3584,128]{1,0:T(8,128)(2,1)} %bitcast.10, bf16[3584,128]{1,0:T(8,128)(2,1)} %bitcast.11, bf16[128,3584]{1,0:T(8,128)(2,1)} %bitcast.12, s32[1,8]{1,0:T(1,128)} %lengths.1, ...), custom_call_target="tpu_custom_call" | custom-call | flops 2818572288 | bytes 6291456 | tf_op jit(solution)/shard_map/pallas_call | solution.py:696
  101.5 1.5 %copy.14 = bf16[8,8,512]{2,1,0:T(8,128)(2,1)} copy(bf16[8,8,512]{2,1,0:T(8,128)(2,1)} %bitcast.8) | data formatting | bytes 131072
  103.0 1.3 %copy.15 = bf16[32,224]{1,0:T(8,128)(2,1)} copy(bf16[32,224]{1,0:T(8,128)(2,1)} %get-tuple-element.9) | data formatting | bytes 28672

commit v9 on v8

--- a/solution.py
+++ b/solution.py
@@ -430,7 +430,7 @@
         return carry
 
     def attend():
-        yield net.now + 8.0
+        yield net.now + 0.3
         loads[0].wait()
         each(lambda j: query_copy(j).wait_recv())
         lat_copy.wait_recv()
@@ -445,7 +445,7 @@
             to = lax.rem(y + j, n_y)
             came.append(net.copy(obuf.at[to], orecv.at[y], (2 * to + c, e), "y"))
         orecv[y] = obuf[y]
-        yield net.now + 25.0
+        yield net.now + 22.0
         for one, _ in came:
             one.wait_recv()
         lax.fori_loop(0, half_req, one_context, 0)
@@ -582,8 +582,7 @@
             experts_of(first, last)
             net.now += 1.0
 
-    attention = attend()
-    net.run([gather_a(), gather_b(), sample(attention, 3), compute()])
+    net.run([gather_a(), gather_b(), compute()])
 
     net.links, net.now = {}, 0.0
     ended = set()
@@ -642,7 +641,7 @@
 
     first_rows = [row_sum(team) for team in reversed(teams)]
     columns = [column_sum(pair) for pair in reversed(pairs)]
-    net.run(first_rows[:1] + columns + first_rows[1:] + [sum_a, sum_b, sample(attention, 9), settle()])
+    net.run(first_rows[:1] + columns + first_rows[1:] + [sum_a, sum_b, attend(), settle()])
 
     for i in range(n_seq):
         begin, turn = share * i // LANE * LANE, share * i % LANE
@@ -663,15 +662,6 @@
     each(lambda j: end_copy(j).wait_send())
     for made in net.copies[len(before):]:
         made.wait_send()
-
-
-def sample(task, most):
-    for _ in range(most):
-        try:
-            ready = next(task)
-        except StopIteration:
-            return
-        yield ready
 
 
 def on_device(latent, lengths, queries, fresh_latent, tokens, routes, gates, w_gate, w_up, w_down):

time: 105 us -> 106 us (level)
    pallas_call x1, Pallas kernels: 101 us -> 102 us  [on_device(): pl.pallas_call(functools.partial(kernel, cfg), out_shape=(jax.ShapeDtypeS...]
where the time goes in v9:
time: 106 us; the launch traced here: 105 us
  Pallas kernels  102 us (96%)
  local copies, waits for them, and re-layouts  2.8 us (3%)
    pallas_call x1, Pallas kernels, on_device(): pl.pallas_call(functools.partial(kernel, cfg), out_shape=(jax.ShapeDtypeS...  102 us
    unnamed x2, local copies, waits for them, and re-layouts  2.8 us

profile of v9, /device:TPU:1, one launch (start us, length us, event | category | flops | bytes accessed | tf_op | source)
XLA Modules:
  0.0 105.4 jit_solution(6760774523389361151)
XLA Ops:
  0.6 102.0 %shard_map.113 = (bf16[64,512]{1,0:T(8,128)(2,1)}, bf16[32,224]{1,0:T(8,128)(2,1)}) custom-call(bf16[8,576,128]{2,1,0:T(8,128)(2,1)} %bitcast.9, bf16[64,576]{1,0:T(8,128)(2,1)} %bitcast.13, bf16[3584,128]{1,0:T(8,128)(2,1)} %bitcast.10, bf16[3584,128]{1,0:T(8,128)(2,1)} %bitcast.11, bf16[128,3584]{1,0:T(8,128)(2,1)} %bitcast.12, s32[1,8]{1,0:T(1,128)} %lengths.1, ...), custom_call_target="tpu_custom_call" | custom-call | flops 2818572288 | bytes 6291456 | tf_op jit(solution)/shard_map/pallas_call | solution.py:686
  102.6 1.5 %copy.14 = bf16[8,8,512]{2,1,0:T(8,128)(2,1)} copy(bf16[8,8,512]{2,1,0:T(8,128)(2,1)} %bitcast.8) | data formatting | bytes 131072
  104.1 1.3 %copy.15 = bf16[32,224]{1,0:T(8,128)(2,1)} copy(bf16[32,224]{1,0:T(8,128)(2,1)} %get-tuple-element.9) | data formatting | bytes 28672

commit v10 on v3

--- a/solution.py
+++ b/solution.py
@@ -169,8 +169,9 @@
     n_req = lengths.shape[1]
     half_req = n_req // 2
     q_rows = half_req * heads
-    x_up, x_down = (s, z * NX + mod(x + 1, NX)), (s, z * NX + mod(x - 1, NX))
-    z_up, z_down = (s, mod(z + 1, n_z) * NX + x), (s, mod(z - 1, n_z) * NX + x)
+    turn = 1 - 2 * c
+    x_up, x_down = (s, z * NX + mod(x + turn, NX)), (s, z * NX + mod(x - turn, NX))
+    z_up, z_down = (s, mod(z + turn, n_z) * NX + x), (s, mod(z - turn, n_z) * NX + x)
     slot_z = {d: i for i, d in enumerate(around(n_z))}
     slot_x = {d: i for i, d in enumerate(around(NX))}
 

time: 103 us -> 103 us (level)
  no operation moved by 1% of the time
where the time goes in v10:
time: 103 us
  Pallas kernels  99.7 us (97%)
  local copies, waits for them, and re-layouts  2.8 us (3%)
    pallas_call x1, Pallas kernels, on_device(): pl.pallas_call(functools.partial(kernel, cfg), out_shape=(jax.ShapeDtypeS...  99.7 us
    unnamed x2, local copies, waits for them, and re-layouts  2.8 us

profile of v10, /device:TPU:1, one launch (start us, length us, event | category | flops | bytes accessed | tf_op | source)
XLA Modules:
  0.0 103.1 jit_solution(5950153473141813073)
XLA Ops:
  0.6 99.7 %shard_map.113 = (bf16[64,512]{1,0:T(8,128)(2,1)}, bf16[32,224]{1,0:T(8,128)(2,1)}) custom-call(bf16[8,576,128]{2,1,0:T(8,128)(2,1)} %bitcast.9, bf16[64,576]{1,0:T(8,128)(2,1)} %bitcast.13, bf16[3584,128]{1,0:T(8,128)(2,1)} %bitcast.10, bf16[3584,128]{1,0:T(8,128)(2,1)} %bitcast.11, bf16[128,3584]{1,0:T(8,128)(2,1)} %bitcast.12, s32[1,8]{1,0:T(1,128)} %lengths.1, ...), custom_call_target="tpu_custom_call" | custom-call | flops 2818572288 | bytes 6291456 | tf_op jit(solution)/shard_map/pallas_call | solution.py:591
  100.3 1.5 %copy.14 = bf16[8,8,512]{2,1,0:T(8,128)(2,1)} copy(bf16[8,8,512]{2,1,0:T(8,128)(2,1)} %bitcast.8) | data formatting | bytes 131072
  101.8 1.3 %copy.15 = bf16[32,224]{1,0:T(8,128)(2,1)} copy(bf16[32,224]{1,0:T(8,128)(2,1)} %get-tuple-element.9) | data formatting | bytes 28672

commit v11 on v8

--- a/solution.py
+++ b/solution.py
@@ -342,14 +342,19 @@
     net = Net(send_sem, recv_sem)
     each(lambda j: token_copy(j).start())
     lat_copy, _ = net.copy(latent.at[pl.ds(other * half_req, half_req)], lbuf.at[1], sibling, "core")
-    weights = [
-        net.copy(src, dst, sibling, "core")[0]
-        for src, dst in (
-            (wg, wcat.at[1]),
-            (wu, wcat.at[3]),
-            (wd, wdcat.at[pl.ds(LANE, LANE)]),
-        )
-    ]
+    for load in loads[1:]:
+        load.wait()
+    weights = []
+    count_w = 7
+    tall, flat = wcat.shape[1] // count_w, LANE // 8
+    for k in range(8):
+        if k < count_w:
+            some = pl.ds(k * tall, tall)
+            weights.append(net.copy(wcat.at[0, some], wcat.at[1, some], sibling, "core")[0])
+            weights.append(net.copy(wcat.at[2, some], wcat.at[3, some], sibling, "core")[0])
+        weights.append(net.copy(
+            wdcat.at[pl.ds(k * flat, flat)], wdcat.at[pl.ds(LANE + k * flat, flat)], sibling, "core"
+        )[0])
     each(lambda j: query_copy(j).start())
 
     tokbuf[s] = tokpad[c]
@@ -575,8 +580,6 @@
             while any(landed[d] < len(pairs) + NX for d in offsets[first:last]):
                 yield net.now + 0.01
             if first == 0:
-                for load in loads[1:]:
-                    load.wait()
                 for made in weights:
                     made.wait_recv()
             experts_of(first, last)
@@ -730,8 +733,8 @@
             pltpu.VMEM((2, q_rows, LAT), BF16),
             pltpu.VMEM((q_rows, LAT), BF16),
             dma((4,)),
-            dma((120,)),
-            dma((120,)),
+            dma((160,)),
+            dma((160,)),
             dma((n_seq,)),
             dma((n_seq,)),
             dma((n_seq,)),

time: 105 us -> 105 us (level)
  no operation moved by 1% of the time
where the time goes in v11:
time: 105 us
  Pallas kernels  102 us (97%)
  local copies, waits for them, and re-layouts  2.8 us (3%)
    pallas_call x1, Pallas kernels, on_device(): pl.pallas_call(functools.partial(kernel, cfg), out_shape=(jax.ShapeDtypeS...  102 us
    unnamed x2, local copies, waits for them, and re-layouts  2.8 us

profile of v11, /device:TPU:1, one launch (start us, length us, event | category | flops | bytes accessed | tf_op | source)
XLA Modules:
  0.0 105.1 jit_solution(10729879569314386351)
XLA Ops:
  0.6 101.6 %shard_map.113 = (bf16[64,512]{1,0:T(8,128)(2,1)}, bf16[32,224]{1,0:T(8,128)(2,1)}) custom-call(bf16[8,576,128]{2,1,0:T(8,128)(2,1)} %bitcast.9, bf16[64,576]{1,0:T(8,128)(2,1)} %bitcast.13, bf16[3584,128]{1,0:T(8,128)(2,1)} %bitcast.10, bf16[3584,128]{1,0:T(8,128)(2,1)} %bitcast.11, bf16[128,3584]{1,0:T(8,128)(2,1)} %bitcast.12, s32[1,8]{1,0:T(1,128)} %lengths.1, ...), custom_call_target="tpu_custom_call" | custom-call | flops 2818572288 | bytes 6291456 | tf_op jit(solution)/shard_map/pallas_call | solution.py:699
  102.3 1.5 %copy.14 = bf16[8,8,512]{2,1,0:T(8,128)(2,1)} copy(bf16[8,8,512]{2,1,0:T(8,128)(2,1)} %bitcast.8) | data formatting | bytes 131072
  103.7 1.3 %copy.15 = bf16[32,224]{1,0:T(8,128)(2,1)} copy(bf16[32,224]{1,0:T(8,128)(2,1)} %get-tuple-element.9) | data formatting | bytes 28672

commit v12 on v3

--- a/solution.py
+++ b/solution.py
@@ -179,21 +179,21 @@
         made.start()
         return made
 
+    barrier = pltpu.get_barrier_semaphore()
+
+    def greet(j, carry):
+        pl.semaphore_signal(
+            barrier, inc=1, device_id=(lax.rem(s + j, n_seq), e), device_id_type=MESH
+        )
+        return carry
+
+    lax.fori_loop(1, n_seq, greet, 0)
+    for who in (x_up, x_down, z_up, z_down):
+        pl.semaphore_signal(barrier, inc=1, device_id=who, device_id_type=MESH)
+
     for half in range(2):
         tokpad[half] = jnp.zeros_like(tokpad[half])
         tokpad[half, :, 0:share] = tokens[half * HALF_TOK:(half + 1) * HALF_TOK, :]
-
-    barrier = pltpu.get_barrier_semaphore()
-
-    def greet(j, carry):
-        pl.semaphore_signal(
-            barrier, inc=1, device_id=(lax.rem(s + j, n_seq), e), device_id_type=MESH
-        )
-        return carry
-
-    lax.fori_loop(1, n_seq, greet, 0)
-    for who in (x_up, x_down, z_up, z_down):
-        pl.semaphore_signal(barrier, inc=1, device_id=who, device_id_type=MESH)
 
     mine_q = queries.at[pl.ds(pl.multiple_of(c * q_rows, q_rows), q_rows)]
     loads = [
@@ -471,7 +471,7 @@
 
     def compute():
         offsets = around(n_z)
-        groups = [(0, 3), (3, 5), (5, 7), (7, 8)] if n_z == 8 else [(0, len(offsets))]
+        groups = [(0, 5), (5, 8)] if n_z == 8 else [(0, len(offsets))]
         for first, last in groups:
             while any(landed[d] < 1 + NX for d in offsets[first:last]):
                 yield net.now + 0.01

time: 103 us -> 105 us (1.019)
  Pallas kernels: 99 us -> 101 us
    pallas_call x1, Pallas kernels: 99 us -> 101 us  [on_device(): pl.pallas_call(functools.partial(kernel, cfg), out_shape=(jax.ShapeDtypeS...]
where the time goes in v12:
time: 105 us; the launch traced here: 104 us
  Pallas kernels  101 us (96%)
  local copies, waits for them, and re-layouts  2.8 us (3%)
    pallas_call x1, Pallas kernels, on_device(): pl.pallas_call(functools.partial(kernel, cfg), out_shape=(jax.ShapeDtypeS...  101 us
    unnamed x2, local copies, waits for them, and re-layouts  2.8 us

profile of v12, /device:TPU:1, one launch (start us, length us, event | category | flops | bytes accessed | tf_op | source)
XLA Modules:
  0.0 104.3 jit_solution(12395297152890657294)
XLA Ops:
  0.6 100.9 %shard_map.113 = (bf16[64,512]{1,0:T(8,128)(2,1)}, bf16[32,224]{1,0:T(8,128)(2,1)}) custom-call(bf16[8,576,128]{2,1,0:T(8,128)(2,1)} %bitcast.9, bf16[64,576]{1,0:T(8,128)(2,1)} %bitcast.13, bf16[3584,128]{1,0:T(8,128)(2,1)} %bitcast.10, bf16[3584,128]{1,0:T(8,128)(2,1)} %bitcast.11, bf16[128,3584]{1,0:T(8,128)(2,1)} %bitcast.12, s32[1,8]{1,0:T(1,128)} %lengths.1, ...), custom_call_target="tpu_custom_call" | custom-call | flops 2818572288 | bytes 6291456 | tf_op jit(solution)/shard_map/pallas_call | solution.py:590
  101.5 1.5 %copy.14 = bf16[8,8,512]{2,1,0:T(8,128)(2,1)} copy(bf16[8,8,512]{2,1,0:T(8,128)(2,1)} %bitcast.8) | data formatting | bytes 131072
  103.0 1.3 %copy.15 = bf16[32,224]{1,0:T(8,128)(2,1)} copy(bf16[32,224]{1,0:T(8,128)(2,1)} %get-tuple-element.9) | data formatting | bytes 28672
